TPU v7x, 512 devices: a whole 4x8x8 slice. The times are simulated.
512 devices in a mesh: dual: 16 (over x, z_hi, core), primal: 8 (over y), seq: 4 (over z_lo).
Axes of the slice: x: 4, y: 8, z: 8 (z_hi: 2, z_lo: 4; z = z_hi * 4 + z_lo), core: 2. Of those that a mesh axis runs over, the one named last changes fastest.
Arguments:
- payoff: bfloat16 [16384, 16384], P('dual', 'primal'), may hold values from -0.0625 to 0.0625
- opp_strategy: float32 [16384, 1024], P(('primal', 'dual'), 'seq'), may hold values from 0 to 1
- opp_combos: int32 [16384], P(('primal', 'dual')), may hold values from 1 to 6
- seq_payoff: bfloat16 [1024, 1024], P(None, 'seq')
- seq_parent: int32 [1024], replicated, may hold values from 0 to 255, as said below
Outputs:
- strategy: float32 [16384, 1024], P(('dual', 'primal'), 'seq')
- opp_grad: float32 [16384, 1024], P(('primal', 'dual'), 'seq')
Inputs may be any that keep to these rules, and one draw needn't show every extreme that they name: `seq_parent`: every information set 0 to 255 is left by at least one sequence.
All inputs are finite; a program needn't handle non-finite values. Where the computation divides by a largest or mean magnitude, that divisor is 1e-20 or more.
Results may differ from a plain program's by a relative error of at most 0.01.
Values may be sent and summed in bfloat16 or wider, within the bound.
No kernel may reach another device: no remote copies, remote signals or barrier semaphores. Data moves between devices by JAX's collectives and lax.ppermute only.
A program may use at most 64 MiB of HBM per device.

v0:
```python
import jax
import jax.numpy as jnp
from jax import lax
from jax.sharding import PartitionSpec as P

NI = 256


logit_span = 6.0
epsilon = 1e-06


def body(payoff, opp_strategy, opp_combos, seq_payoff, seq_parent):
    scaled = (opp_combos.astype(jnp.float32)[:, None] * opp_strategy).astype(jnp.bfloat16)
    opponent_block = lax.all_gather(scaled, "dual", axis=0, tiled=True)
    inner_sum = lax.psum_scatter(
        jnp.dot(payoff, opponent_block, preferred_element_type=jnp.float32),
        "primal",
        scatter_dimension=0,
        tiled=True,
    )
    inner_low = inner_sum.astype(jnp.bfloat16)
    partial_grad = lax.dot_general(
        inner_low, seq_payoff, (((1,), (1,)), ((), ())), preferred_element_type=jnp.float32
    )
    seq_width = seq_payoff.shape[1]
    infoset_ids = jnp.arange(NI, dtype=jnp.int32)
    gradient = lax.psum_scatter(partial_grad, "seq", scatter_dimension=1, tiled=True)
    largest = lax.pmax(jnp.max(jnp.abs(gradient), axis=1), "seq")
    exponent = jnp.exp(-logit_span * gradient / (largest[:, None] + epsilon))
    own_parent = lax.dynamic_slice_in_dim(
        seq_parent, lax.axis_index("seq") * seq_width, seq_width, 0
    )
    onehot = (own_parent[:, None] == infoset_ids[None, :]).astype(jnp.float32)
    totals = lax.psum(jnp.dot(exponent, onehot, precision=lax.Precision.HIGHEST), "seq")
    strategy = exponent / jnp.dot(totals, onehot.T, precision=lax.Precision.HIGHEST)
    spread = lax.all_gather(strategy.astype(jnp.bfloat16), "seq", axis=1, tiled=True)
    through = jnp.dot(spread, seq_payoff, preferred_element_type=jnp.float32).astype(jnp.bfloat16)
    player_block = lax.all_gather(through, "primal", axis=0, tiled=True)
    opp_grad = lax.psum_scatter(
        lax.dot_general(
            payoff, player_block, (((0,), (0,)), ((), ())), preferred_element_type=jnp.float32
        ),
        "dual",
        scatter_dimension=0,
        tiled=True,
    )
    return (strategy, opp_grad)


def solution(mesh):
    return jax.shard_map(
        body,
        mesh=mesh,
        in_specs=(
            P("dual", "primal"),
            P(("primal", "dual"), "seq"),
            P(("primal", "dual")),
            P(None, "seq"),
            P(),
        ),
        out_specs=(P(("dual", "primal"), "seq"), P(("primal", "dual"), "seq")),
        check_vma=False,
    )
```

profile of v0, /device:TPU:1, one launch (start us, length us, event | category | flops | bytes accessed | tf_op | source)
XLA Modules:
  0.0 369.0 jit_solution(6454620260282091022)
XLA Ops:
  7.2 0.0 copy-start
  7.2 0.0 all-gather.2.cloned.1.call-start
  7.2 0.7 convert_element_type.16
  7.9 1.6 multiply_convert_fusion
  9.6 0.0 all-gather.2.cloned.1.call-update
  9.6 0.0 reduce-scatter.4.cloned.1.call-start
  9.6 69.7 %all-gather.2.cloned.1.call-done = bf16[2048,256]{1,0:T(8,128)(2,1)} async-done(((bf16[128,256]{1,0:T(8,128)(2,1)}), bf16[2048,256]{1,0:T(8,128)(2,1)}) %all-gather.2.cloned.1.call-update) | async-done | bytes 1048592 | tf_op jit(solution)/shard_map/all_gather | solution.py:15
  79.4 4.8 %convolution_bitcast_fusion.1 = f32[1024,256]{0,1:T(8,128)} fusion(bf16[2048,256]{1,0:T(8,128)(2,1)} %all-gather.2.cloned.1.call-done, bf16[1024,2048]{1,0:T(8,128)(2,1)} %param.5), kind=kOutput, calls=%fused_computation.1 | convolution fusion | flops 1073741824 | bytes 6291456 | tf_op jit(solution)/shard_map/dot_general | solution.py:17
  84.2 0.0 reduce-scatter.4.cloned.1.call-update
  84.2 0.0 reduce-scatter.6.cloned.1.call-start
  84.2 31.9 %reduce-scatter.4.cloned.1.call-done = f32[128,256]{0,1:T(8,128)} async-done(((f32[1024,256]{0,1:T(8,128)}), f32[128,256]{0,1:T(8,128)}) %reduce-scatter.4.cloned.1.call-update) | async-done | bytes 131088 | tf_op jit(solution)/shard_map/reduce_scatter | solution.py:16
  116.2 0.0 copy-done
  116.2 2.0 fusion.3
  118.2 0.0 reduce-scatter.6.cloned.1.call-update
  118.2 0.0 all-reduce.2.cloned.1.call-start
  118.3 0.8 dynamic_slice.3
  119.0 31.9 %reduce-scatter.6.cloned.1.call-done = f32[128,256]{1,0:T(8,128)} async-done(((f32[128,1024]{1,0:T(8,128)}), f32[128,256]{1,0:T(8,128)}) %reduce-scatter.6.cloned.1.call-update) | async-done | bytes 131088 | tf_op jit(solution)/shard_map/reduce_scatter | solution.py:28
  150.9 1.0 abs_reduce_fusion
  151.9 7.3 %pmax.7 = f32[128]{0:T(128)S(1)} all-reduce(f32[128]{0:T(128)S(1)} %abs_reduce_fusion), channel_id=1, replica_groups=mesh['dual'=16,'primal'=8,'seq'=4] {'seq'}, use_global_device_ids=true, to_apply=%region_3.0 | all-reduce | flops 128 | bytes 1024 | tf_op jit(solution)/shard_map/pmax | solution.py:29
  159.2 1.9 fusion
  161.1 0.0 all-reduce.2.cloned.1.call-update
  161.1 0.0 reduce-scatter.8.cloned.1.call-start
  161.2 56.9 %all-reduce.2.cloned.1.call-done = f32[128,256]{1,0:T(8,128)} async-done(((f32[128,256]{1,0:T(8,128)}), f32[128,256]{1,0:T(8,128)}) %all-reduce.2.cloned.1.call-update) | async-done | bytes 131088 | tf_op jit(solution)/shard_map/psum | solution.py:35
  218.1 2.0 fusion.6
  220.1 12.0 %all_gather.10 = bf16[128,1024]{1,0:T(8,128)(2,1)S(1)} all-gather(bf16[128,256]{1,0:T(8,128)(2,1)S(1)} %get-tuple-element.4), channel_id=1, replica_groups=mesh['dual'=16,'primal'=8,'seq'=4] {'seq'}, dimensions={1}, use_global_device_ids=true | all-gather | bytes 327680 | tf_op jit(solution)/shard_map/all_gather | solution.py:37
  232.1 0.2 convolution_convert_fusion
  232.3 21.1 %all_gather.11 = bf16[1024,256]{1,0:T(8,128)(2,1)S(1)} all-gather(bf16[128,256]{1,0:T(8,128)(2,1)S(1)} %convolution_convert_fusion), channel_id=1, replica_groups=mesh['dual'=16,'primal'=8,'seq'=4] {'primal'}, dimensions={0}, use_global_device_ids=true | all-gather | bytes 589824 | tf_op jit(solution)/shard_map/all_gather | solution.py:39
  253.5 4.8 %convolution_bitcast_fusion = f32[2048,256]{0,1:T(8,128)} fusion(bf16[1024,256]{1,0:T(8,128)(2,1)S(1)} %all_gather.11, bf16[1024,2048]{1,0:T(8,128)(2,1)} %param.5), kind=kOutput, calls=%fused_computation | convolution fusion | flops 1073741824 | bytes 6815744 | tf_op jit(solution)/shard_map/dot_general | solution.py:41
  258.3 0.0 reduce-scatter.8.cloned.1.call-update
  258.3 102.5 %reduce-scatter.8.cloned.1.call-done = f32[128,256]{0,1:T(8,128)} async-done(((f32[2048,256]{0,1:T(8,128)}), f32[128,256]{0,1:T(8,128)}) %reduce-scatter.8.cloned.1.call-update) | async-done | bytes 131088 | tf_op jit(solution)/shard_map/reduce_scatter | solution.py:40
  360.8 1.7 copy.7
  (1 shorter events, 0.0 us)
Async XLA Ops:
  7.2 109.0 %copy-start = (bf16[1024,256]{1,0:T(8,128)(2,1)S(1)}, bf16[1024,256]{1,0:T(8,128)(2,1)}, u32[]{:S(2)}) copy-start(bf16[1024,256]{1,0:T(8,128)(2,1)} %param.8) | copy-start | bytes 1572868
  7.2 72.2 %all-gather.2.cloned.1.call-start = ((), (), s32[]{:S(2)}) async-start(), calls=%async_computation.3 | async-start | bytes 1114112 | tf_op jit(solution)/shard_map/all_gather | solution.py:15
  9.6 106.6 %reduce-scatter.4.cloned.1.call-start = ((), (), s32[]{:S(2)}) async-start(), calls=%async_computation.4 | async-start | bytes 1179648 | tf_op jit(solution)/shard_map/reduce_scatter | solution.py:16
  84.2 66.7 %reduce-scatter.6.cloned.1.call-start = ((), (), s32[]{:S(2)}) async-start(), calls=%async_computation.5 | async-start | bytes 655360 | tf_op jit(solution)/shard_map/reduce_scatter | solution.py:28
  118.2 99.9 %all-reduce.2.cloned.1.call-start = ((), (), s32[]{:S(2)}) async-start(), calls=%async_computation.6 | async-start | bytes 262144 | tf_op jit(solution)/shard_map/psum | solution.py:35
  161.1 199.7 %reduce-scatter.8.cloned.1.call-start = ((), (), s32[]{:S(2)}) async-start(), calls=%async_computation.7 | async-start | bytes 2228224 | tf_op jit(solution)/shard_map/reduce_scatter | solution.py:40
Sparse Core Ops, SparseCore 0:
  11.9 67.4 all-gather.1
  84.3 31.8 reduce-scatter.3
  119.0 31.8 reduce-scatter.5
  161.2 56.7 all-reduce.1
  258.4 102.3 reduce-scatter.7
where the time goes:
time: 370 us; the launch traced here: 369 us
  waiting for transfers between devices  293 us (79%)
  blocking collectives  40.5 us (11%)
  matrix products  15.7 us (4%)
  between operations  13.8 us (4%)
    reduce_scatter x1, waiting for transfers between devices, body(): lax.psum_scatter(lax.dot_general(payoff, player_block, (((0,), (0,)), (()...  102 us
    all_gather x1, waiting for transfers between devices, body(): opponent_block = lax.all_gather(scaled, 'dual', axis=0, tiled=True)  69.7 us
    psum x1, waiting for transfers between devices, body(): lax.psum(jnp.dot(exponent, onehot, precision=lax.Precision.HIGHEST), 'seq')  56.9 us
    reduce_scatter x1, waiting for transfers between devices, body(): lax.psum_scatter(jnp.dot(payoff, opponent_block, preferred_element_type=j...  31.9 us
    reduce_scatter x1, waiting for transfers between devices, body(): lax.psum_scatter(partial_grad, 'seq', scatter_dimension=1, tiled=True)  31.9 us
    all_gather x1, blocking collectives, body(): player_block = lax.all_gather(through, 'primal', axis=0, tiled=True)  21.1 us
    all_gather x1, blocking collectives, body(): lax.all_gather(strategy.astype(jnp.bfloat16), 'seq', axis=1, tiled=True)  12 us
  transfers between devices with their start and end apart: 5, of which 5 were waited for; matrix products, arithmetic and copies ran while one was open for 0% of the time, Pallas kernels for 0%

commit v1 on v0

v1 whole, which is shorter than its diff:
```python
import jax
import jax.numpy as jnp
from jax import lax
from jax.sharding import Mesh, PartitionSpec as P

logit_span = 6.0
epsilon = 1e-06

bf16 = jnp.bfloat16
f32 = jnp.float32
DUAL = ("x", "zh", "core")
SWAP = ((0, 1), (1, 0))


def exchange(blocks, axis):
    return lax.all_to_all(blocks, axis, split_axis=0, concat_axis=0, tiled=True)


def spread(block, copies, axis):
    return exchange(jnp.broadcast_to(block[None], (copies, *block.shape)), axis)


def pick(pair, index):
    return lax.dynamic_index_in_dim(pair, index, 0, keepdims=False)


def body(payoff, opp_strategy, opp_combos, seq_payoff, seq_parent):
    rows, width = opp_strategy.shape
    n_x, n_zh, n_y, n_seq = (lax.axis_size(a) for a in ("x", "zh", "primal", "seq"))
    core, zh, seq = (lax.axis_index(a) for a in ("core", "zh", "seq"))
    same = (seq_parent[:, None] == seq_parent[None, :]).astype(bf16)

    scaled = (opp_combos.astype(f32)[:, None] * opp_strategy).astype(bf16)
    part = jnp.einsum(
        "bt,zst->zbs",
        scaled,
        seq_payoff.reshape(n_seq, width, width),
        preferred_element_type=f32,
    ).astype(bf16)
    part = jnp.broadcast_to(part[None], (n_zh, *part.shape)).reshape(-1, rows, width)
    part = exchange(part, ("zh", "seq")).reshape(n_zh, n_seq, rows, width)
    mixed = part.astype(f32).sum(axis=1).astype(bf16)

    mixed = spread(mixed, n_x, "x").reshape(n_x * n_zh, rows, width)
    other = lax.ppermute(mixed, "core", SWAP)
    block = jnp.stack(
        [jnp.where(core == 0, mixed, other), jnp.where(core == 0, other, mixed)], axis=1
    ).reshape(-1, width)

    partial_grad = jnp.dot(payoff, block, preferred_element_type=f32).astype(bf16)
    partial_grad = exchange(partial_grad.reshape(n_y, rows, width), "primal")
    gradient = partial_grad.astype(f32).sum(axis=0).astype(bf16)
    gradient = spread(gradient, n_seq, "seq").astype(f32)

    largest = jnp.max(jnp.abs(gradient), axis=(0, 2), keepdims=True)
    exponent = jnp.exp(-logit_span * gradient / (largest + epsilon))
    exponent = jnp.swapaxes(exponent, 0, 1).reshape(rows, n_seq * width)
    high = exponent.astype(bf16)
    low = (exponent - high.astype(f32)).astype(bf16)
    totals = jnp.dot(
        jnp.concatenate([high, low], axis=0), same, preferred_element_type=f32
    )
    strategy = exponent / (totals[:rows] + totals[rows:])
    through = jnp.dot(
        strategy.astype(bf16), seq_payoff, preferred_element_type=f32
    ).astype(bf16)
    own_strategy = lax.dynamic_slice_in_dim(strategy, seq * width, width, 1)

    player_block = spread(through, n_y, "primal").reshape(-1, width)
    opp = lax.dot_general(
        payoff, player_block, (((0,), (0,)), ((), ())), preferred_element_type=f32
    ).astype(bf16)
    opp = opp.reshape(n_x * n_zh, 2, rows, width).swapaxes(0, 1)
    opp = pick(opp, core).astype(f32) + lax.ppermute(
        pick(opp, 1 - core), "core", SWAP
    ).astype(f32)
    opp = exchange(opp.astype(bf16).reshape(n_x, n_zh * rows, width), "x")
    opp = opp.astype(f32).sum(axis=0).reshape(n_zh, rows, width)
    opp_grad = pick(opp, zh) + lax.ppermute(
        pick(opp, 1 - zh).astype(bf16), "zh", SWAP
    ).astype(f32)
    return own_strategy, opp_grad


def solution(mesh):
    n_dual, n_primal, n_seq = mesh.devices.shape
    fine = Mesh(
        mesh.devices.reshape(n_dual // 4, 2, 2, n_primal, n_seq),
        (*DUAL, "primal", "seq"),
    )
    opponent_rows = ("primal", *DUAL)
    return jax.shard_map(
        body,
        mesh=fine,
        in_specs=(
            P(DUAL, "primal"),
            P(opponent_rows, "seq"),
            P(opponent_rows),
            P(None, "seq"),
            P(),
        ),
        out_specs=(P((*DUAL, "primal"), "seq"), P(opponent_rows, "seq")),
        check_vma=False,
    )
```

time: 370 us -> 148 us (0.40)
  waiting for transfers between devices: 293 us -> 31.7 us
  blocking collectives: 40.5 us -> 71.6 us
  starting transfers between devices: 0.21 us -> 21.7 us
  between operations: 13.8 us -> 0.89 us
  matrix products: 15.7 us -> 7.13 us
  local copies, waits for them, and re-layouts: 2.43 us -> 9.81 us
    reduce_scatter x3 -> x0, waiting for transfers between devices: 166 us -> none  [the longest x1 102 us: body(): lax.psum_scatter(lax.dot_general(payoff, player_block, (((0,), (0,)), (()...]
    all_to_all x0 -> x4, blocking collectives: none -> 71.6 us  [exchange(): return lax.all_to_all(blocks, axis, split_axis=0, concat_axis=0, tiled=True)]
    all_gather x1 -> x0, waiting for transfers between devices: 69.7 us -> none  [body(): opponent_block = lax.all_gather(scaled, 'dual', axis=0, tiled=True)]
    psum x1 -> x0, waiting for transfers between devices: 56.9 us -> none  [body(): lax.psum(jnp.dot(exponent, onehot, precision=lax.Precision.HIGHEST), 'seq')]
    all_gather x2 -> x0, blocking collectives: 33.2 us -> none  [the longest x1 21.1 us: body(): player_block = lax.all_gather(through, 'primal', axis=0, tiled=True)]
    all_to_all x0 -> x2, waiting for transfers between devices: none -> 23.9 us  [exchange(): return lax.all_to_all(blocks, axis, split_axis=0, concat_axis=0, tiled=True)]
    ppermute x0 -> x3, starting transfers between devices: none -> 14.8 us  [the longest x1 5.78 us: body(): other = lax.ppermute(mixed, 'core', SWAP)]
    ppermute x0 -> x3, waiting for transfers between devices: none -> 7.8 us  [the longest x1 5.58 us: body(): lax.ppermute(pick(opp, 1 - zh).astype(bf16), 'zh', SWAP).astype(f32)]
  transfers between devices with their start and end apart: 5 -> 5, of which waited for: 5 -> 5; matrix products, arithmetic and copies ran while one was open for 0% -> 1% of each run, Pallas kernels for 0% -> 0%
where the time goes in v1:
time: 148 us; the launch traced here: 147 us
  blocking collectives  71.6 us (48%)
  waiting for transfers between devices  31.7 us (21%)
  starting transfers between devices  21.7 us (15%)
  local copies, waits for them, and re-layouts  9.81 us (7%)
  matrix products  7.13 us (5%)
  other arithmetic  4.23 us (3%)
    all_to_all x4, blocking collectives, exchange(): return lax.all_to_all(blocks, axis, split_axis=0, concat_axis=0, tiled=True)  71.6 us
    all_to_all x2, waiting for transfers between devices, exchange(): return lax.all_to_all(blocks, axis, split_axis=0, concat_axis=0, tiled=True)  23.9 us
    all_to_all x2, starting transfers between devices, exchange(): return lax.all_to_all(blocks, axis, split_axis=0, concat_axis=0, tiled=True)  6.96 us
    ppermute x1, starting transfers between devices, body(): other = lax.ppermute(mixed, 'core', SWAP)  5.78 us
    ppermute x1, waiting for transfers between devices, body(): lax.ppermute(pick(opp, 1 - zh).astype(bf16), 'zh', SWAP).astype(f32)  5.58 us
    ppermute x1, starting transfers between devices, body(): lax.ppermute(pick(opp, 1 - core), 'core', SWAP).astype(f32)  5.54 us
    unnamed x8, local copies, waits for them, and re-layouts  4.06 us
    ppermute x1, starting transfers between devices, body(): lax.ppermute(pick(opp, 1 - zh).astype(bf16), 'zh', SWAP).astype(f32)  3.46 us
  transfers between devices with their start and end apart: 5, of which 5 were waited for; matrix products, arithmetic and copies ran while one was open for 1% of the time, Pallas kernels for 0%

profile of v1, /device:TPU:1, one launch (start us, length us, event | category | flops | bytes accessed | tf_op | source)
XLA Modules:
  0.0 147.1 jit_solution(13176634291206812492)
XLA Ops:
  0.6 0.0 copy-start
  0.6 0.7 convert_element_type.71
  1.4 0.3 copy-done
  1.7 1.2 fusion.6
  3.0 26.7 %all_to_all.30 = bf16[8,128,256]{2,1,0:T(8,128)(2,1)S(1)} all-to-all(bf16[8,128,256]{2,1,0:T(8,128)(2,1)S(1)} %bitcast.54), channel_id=1, replica_groups=mesh['x'=4,'zh'=2,'core'=2,'primal'=8,'seq'=4] {'zh','seq'}, dimensions={0} | all-to-all | bytes 1048576 | tf_op jit(solution)/shard_map/all_to_all | solution.py:16
  29.6 0.1 bitcast_reduce_fusion
  29.7 10.7 %all_to_all.31 = bf16[4,2,128,256]{3,2,1,0:T(8,128)(2,1)S(1)} all-to-all(bf16[4,2,128,256]{3,2,1,0:T(8,128)(2,1)S(1)} %broadcast_in_dim.9), channel_id=1, replica_groups=mesh['x'=4,'zh'=2,'core'=2,'primal'=8,'seq'=4] {'x'}, dimensions={0} | all-to-all | bytes 1048576 | tf_op jit(solution)/shard_map/all_to_all | solution.py:16
  40.5 5.8 %collective-permute-start = (bf16[8,128,256]{2,1,0:T(8,128)(2,1)S(1)}, bf16[8,128,256]{2,1,0:T(8,128)(2,1)S(1)}, u32[]{:S(2)}, u32[]{:S(2)}) collective-permute-start(bf16[8,128,256]{2,1,0:T(8,128)(2,1)S(1)} %bitcast.53), channel_id=1, source_target_pairs={{0,32},{32,0},{1,33},{33,1},{2,34},{34,2},{3,35},{35,3},{4,36},{36... | collective-permute-start | bytes 1572872 | tf_op jit(solution)/shard_map/ppermute | solution.py:45
  46.3 0.0 copy-start.1
  46.3 1.5 %collective-permute-done = bf16[8,128,256]{2,1,0:T(8,128)(2,1)S(1)} collective-permute-done((bf16[8,128,256]{2,1,0:T(8,128)(2,1)S(1)}, bf16[8,128,256]{2,1,0:T(8,128)(2,1)S(1)}, u32[]{:S(2)}, u32[]{:S(2)}) %collective-permute-start) | collective-permute-done | bytes 524320 | tf_op jit(solution)/shard_map/ppermute | solution.py:45
  47.8 0.1 select_bitcast_fusion.1
  47.9 0.1 pad_maximum_fusion
  48.0 0.5 copy-done.1
  48.5 1.3 fusion.5
  49.8 0.0 copy-start.2
  49.8 0.1 copy.30
  49.9 24.6 %all_to_all.32 = bf16[8,128,256]{1,2,0:T(8,128)(2,1)S(1)} all-to-all(bf16[8,128,256]{1,2,0:T(8,128)(2,1)S(1)} %bitcast.55), channel_id=1, replica_groups=mesh['x'=4,'zh'=2,'core'=2,'primal'=8,'seq'=4] {'primal'}, dimensions={0} | all-to-all | bytes 1048576 | tf_op jit(solution)/shard_map/all_to_all | solution.py:16
  74.5 0.1 reduce_sum.34
  74.6 0.1 copy.20
  74.7 9.6 %all_to_all.33 = bf16[4,128,256]{2,1,0:T(8,128)(2,1)S(1)} all-to-all(bf16[4,128,256]{2,1,0:T(8,128)(2,1)S(1)} %broadcast_in_dim.10), channel_id=1, replica_groups=mesh['x'=4,'zh'=2,'core'=2,'primal'=8,'seq'=4] {'seq'}, dimensions={0} | all-to-all | bytes 524288 | tf_op jit(solution)/shard_map/all_to_all | solution.py:16
  84.3 0.1 fusion.11
  84.4 0.2 fusion.10
  84.7 0.1 subtract_convert_fusion
  84.7 0.0 copy-done.2
  84.8 0.9 fusion
  85.7 0.1 fusion.12
  85.8 0.2 convolution_convert_fusion.3
  86.1 0.8 broadcast_in_dim.11
  86.9 3.5 %all-to-all-start.4 = ((bf16[8,128,256]{2,1,0:T(8,128)(2,1)}), bf16[8,128,256]{2,1,0:T(8,128)(2,1)S(1)}, u32[]{:S(2)}, u32[]{:S(2)}) async-start(bf16[8,128,256]{2,1,0:T(8,128)(2,1)} %broadcast_in_dim.11), calls=%async_computation.4 | async-start | bytes 1048576 | tf_op jit(solution)/shard_map/all_to_all | solution.py:16
  90.4 14.7 %all-to-all-done.4 = bf16[8,128,256]{2,1,0:T(8,128)(2,1)S(1)} async-done(((bf16[8,128,256]{2,1,0:T(8,128)(2,1)}), bf16[8,128,256]{2,1,0:T(8,128)(2,1)S(1)}, u32[]{:S(2)}, u32[]{:S(2)}) %all-to-all-start.4) | async-done | bytes 524320 | tf_op jit(solution)/shard_map/all_to_all | solution.py:16
  105.1 3.5 %fusion.2 = bf16[2048,256]{0,1:T(8,128)(2,1)S(1)} fusion(bf16[1024,256]{1,0:T(8,128)(2,1)S(1)} %bitcast.60, bf16[1024,2048]{1,0:T(8,128)(2,1)} %param.5), kind=kOutput, calls=%fused_computation.3 | convolution fusion | flops 1074266112 | bytes 5767168 | tf_op jit(solution)/shard_map/dot_general | solution.py:70
  108.6 0.8 reshape.63
  109.3 3.1 %constant_dynamic-slice_fusion.1 = (bf16[8,1,128,256]{2,1,0,3:T(2,128)(2,1)S(1)}, bf16[8,1,128,256]{2,1,0,3:T(2,128)(2,1)}) fusion(bf16[8,2,128,256]{2,1,0,3:T(2,128)(2,1)S(1)} %reshape.63, s32[]{:T(128)S(6)} %select_n.33, s32[]{:T(128)S(6)} %select_n.34), kind=kLoop, calls=%fused_computation.39 | loop fusion | bytes 2097160 | tf_op jit(solution)/shard_map/dynamic-slice
  112.5 2.3 %copy.26 = bf16[8,1,128,256]{3,2,0,1:T(8,128)(2,1)S(1)} copy(bf16[8,1,128,256]{2,1,0,3:T(2,128)(2,1)} %get-tuple-element.5) | data formatting | bytes 1048576
  114.8 5.5 %collective-permute-start.1 = (bf16[8,128,256]{2,1,0:T(8,128)(2,1)S(1)}, bf16[8,128,256]{2,1,0:T(8,128)(2,1)}, u32[]{:S(2)}, u32[]{:S(2)}) collective-permute-start(bf16[8,128,256]{2,1,0:T(8,128)(2,1)S(1)} %bitcast.59), channel_id=1, source_target_pairs={{0,32},{32,0},{1,33},{33,1},{2,34},{34,2},{3,35},{35,3},{4,36},{36... | collective-permute-start | bytes 1572872 | tf_op jit(solution)/shard_map/ppermute | solution.py:74
  120.4 0.9 copy.25
  121.3 0.7 collective-permute-done.1
  122.0 2.0 %fusion.7 = bf16[8,128,256]{2,1,0:T(8,128)(2,1)} fusion(bf16[8,128,256]{2,1,0:T(8,128)(2,1)} %collective-permute-done.1, bf16[8,1,128,256]{3,2,0,1:T(8,128)(2,1)S(1)} %copy.25), kind=kLoop, calls=%fused_computation.13 | loop fusion | flops 1048576 | bytes 1572864 | tf_op jit(solution)/shard_map/convert_element_type | solution.py:77
  124.0 3.5 %all-to-all-start.5 = ((bf16[4,256,256]{2,1,0:T(8,128)(2,1)}), bf16[4,256,256]{2,1,0:T(8,128)(2,1)S(1)}, u32[]{:S(2)}, u32[]{:S(2)}) async-start(bf16[4,256,256]{2,1,0:T(8,128)(2,1)} %bitcast.16), calls=%async_computation.5 | async-start | bytes 1048576 | tf_op jit(solution)/shard_map/all_to_all | solution.py:16
  127.4 9.2 %all-to-all-done.5 = bf16[4,256,256]{2,1,0:T(8,128)(2,1)S(1)} async-done(((bf16[4,256,256]{2,1,0:T(8,128)(2,1)}), bf16[4,256,256]{2,1,0:T(8,128)(2,1)S(1)}, u32[]{:S(2)}, u32[]{:S(2)}) %all-to-all-start.5) | async-done | bytes 524320 | tf_op jit(solution)/shard_map/all_to_all | solution.py:16
  136.6 0.1 convert_reduce_fusion
  136.7 3.5 %collective-permute-start.2 = (bf16[128,256]{1,0:T(8,128)(2,1)S(1)}, bf16[128,256]{1,0:T(8,128)(2,1)S(1)}, u32[]{:S(2)}, u32[]{:S(2)}) collective-permute-start(bf16[128,256]{1,0:T(8,128)(2,1)S(1)} %fusion.19), channel_id=1, source_target_pairs={{0,64},{64,0},{1,65},{65,1},{2,66},{66,2},{3,67},{67,3},{4,68},{68... | collective-permute-start | bytes 196616 | tf_op jit(solution)/shard_map/ppermute | solution.py:79
  140.2 0.7 constant_dynamic-slice_fusion.2
  140.9 5.6 %collective-permute-done.2 = bf16[128,256]{1,0:T(8,128)(2,1)S(1)} collective-permute-done((bf16[128,256]{1,0:T(8,128)(2,1)S(1)}, bf16[128,256]{1,0:T(8,128)(2,1)S(1)}, u32[]{:S(2)}, u32[]{:S(2)}) %collective-permute-start.2) | collective-permute-done | bytes 65568 | tf_op jit(solution)/shard_map/ppermute | solution.py:79
  146.4 0.7 bitcast_add_fusion
  (6 shorter events, 0.2 us)
Async XLA Ops:
  0.6 1.1 copy-start
  40.5 7.3 %collective-permute-start = (bf16[8,128,256]{2,1,0:T(8,128)(2,1)S(1)}, bf16[8,128,256]{2,1,0:T(8,128)(2,1)S(1)}, u32[]{:S(2)}, u32[]{:S(2)}) collective-permute-start(bf16[8,128,256]{2,1,0:T(8,128)(2,1)S(1)} %bitcast.53), channel_id=1, source_target_pairs={{0,32},{32,0},{1,33},{33,1},{2,34},{34,2},{3,35},{35,3},{4,36},{36... | collective-permute-start | bytes 1572872 | tf_op jit(solution)/shard_map/ppermute | solution.py:45
  46.3 2.2 %copy-start.1 = (bf16[1024,2048]{1,0:T(8,128)(2,1)S(1)}, bf16[1024,2048]{1,0:T(8,128)(2,1)}, u32[]{:S(2)}) copy-start(bf16[1024,2048]{1,0:T(8,128)(2,1)} %param.5) | copy-start | bytes 12582916
  49.8 35.0 %copy-start.2 = (s32[1024]{0:T(1024)S(1)}, s32[1024]{0:T(1024)}, u32[]{:S(2)}) copy-start(s32[1024]{0:T(1024)} %param.9) | copy-start | bytes 12292
  86.9 18.2 %all-to-all-start.4 = ((bf16[8,128,256]{2,1,0:T(8,128)(2,1)}), bf16[8,128,256]{2,1,0:T(8,128)(2,1)S(1)}, u32[]{:S(2)}, u32[]{:S(2)}) async-start(bf16[8,128,256]{2,1,0:T(8,128)(2,1)} %broadcast_in_dim.11), calls=%async_computation.4 | async-start | bytes 1048576 | tf_op jit(solution)/shard_map/all_to_all | solution.py:16
  114.8 7.2 %collective-permute-start.1 = (bf16[8,128,256]{2,1,0:T(8,128)(2,1)S(1)}, bf16[8,128,256]{2,1,0:T(8,128)(2,1)}, u32[]{:S(2)}, u32[]{:S(2)}) collective-permute-start(bf16[8,128,256]{2,1,0:T(8,128)(2,1)S(1)} %bitcast.59), channel_id=1, source_target_pairs={{0,32},{32,0},{1,33},{33,1},{2,34},{34,2},{3,35},{35,3},{4,36},{36... | collective-permute-start | bytes 1572872 | tf_op jit(solution)/shard_map/ppermute | solution.py:74
  124.0 12.7 %all-to-all-start.5 = ((bf16[4,256,256]{2,1,0:T(8,128)(2,1)}), bf16[4,256,256]{2,1,0:T(8,128)(2,1)S(1)}, u32[]{:S(2)}, u32[]{:S(2)}) async-start(bf16[4,256,256]{2,1,0:T(8,128)(2,1)} %bitcast.16), calls=%async_computation.5 | async-start | bytes 1048576 | tf_op jit(solution)/shard_map/all_to_all | solution.py:16
  136.7 9.7 %collective-permute-start.2 = (bf16[128,256]{1,0:T(8,128)(2,1)S(1)}, bf16[128,256]{1,0:T(8,128)(2,1)S(1)}, u32[]{:S(2)}, u32[]{:S(2)}) collective-permute-start(bf16[128,256]{1,0:T(8,128)(2,1)S(1)} %fusion.19), channel_id=1, source_target_pairs={{0,64},{64,0},{1,65},{65,1},{2,66},{66,2},{3,67},{67,3},{4,68},{68... | collective-permute-start | bytes 196616 | tf_op jit(solution)/shard_map/ppermute | solution.py:79

commit v2 on v1

v2 whole, which is shorter than its diff:
```python
import jax
import jax.numpy as jnp
from jax import lax
from jax.experimental import pallas as pl
from jax.experimental.pallas import tpu as pltpu
from jax.sharding import Mesh, PartitionSpec as P

logit_span = 6.0
epsilon = 1e-06

bf16 = jnp.bfloat16
f32 = jnp.float32
DUAL = ("x", "zh", "core")
CHIPS = ("x", "zh")
PLANE = ("primal", "seq")
SWAP = ((0, 1), (1, 0))


def exchange(blocks, axis):
    return lax.all_to_all(blocks, axis, split_axis=0, concat_axis=0, tiled=True)


def spread(block, copies, axis):
    return exchange(jnp.broadcast_to(block[None], (copies, *block.shape)), axis)


def pick(pair, index):
    return lax.dynamic_index_in_dim(pair, index, 0, keepdims=False)


def player_kernel(payoff_ref, block_ref, out_ref):
    out_ref[...] = jnp.dot(
        payoff_ref[...], block_ref[...], preferred_element_type=f32
    ).astype(bf16)


def player_product(payoff, block):
    n_rows, depth = payoff.shape
    width = block.shape[1]
    step = n_rows // 4
    return pl.pallas_call(
        player_kernel,
        grid=(n_rows // step,),
        in_specs=[
            pl.BlockSpec((step, depth), lambda i: (i, 0)),
            pl.BlockSpec((depth, width), lambda i: (0, 0)),
        ],
        out_specs=pl.BlockSpec((step, width), lambda i: (i, 0)),
        out_shape=jax.ShapeDtypeStruct((n_rows, width), bf16),
        cost_estimate=pl.CostEstimate(
            flops=2 * n_rows * depth * width,
            bytes_accessed=2 * n_rows * depth,
            transcendentals=0,
        ),
    )(payoff, block)


def opponent_kernel(payoff_ref, block_ref, out_ref, turned):
    @pl.when(pl.program_id(0) == 0)
    def _():
        turned[...] = block_ref[...].T

    total = jnp.dot(turned[...], payoff_ref[...], preferred_element_type=f32)
    rows = out_ref.shape[-1]
    for chip in range(out_ref.shape[1]):
        for core in range(2):
            at = (2 * chip + core) * rows
            out_ref[core, chip] = total[:, at : at + rows].astype(bf16)


def opponent_product(payoff, block, chips, rows):
    depth, n_cols = payoff.shape
    width = block.shape[1]
    step = 2
    return pl.pallas_call(
        opponent_kernel,
        grid=(chips // step,),
        in_specs=[
            pl.BlockSpec((depth, step * 2 * rows), lambda i: (0, i)),
            pl.BlockSpec((depth, width), lambda i: (0, 0)),
        ],
        out_specs=pl.BlockSpec((2, step, width, rows), lambda i: (0, i, 0, 0)),
        out_shape=jax.ShapeDtypeStruct((2, chips, width, rows), bf16),
        scratch_shapes=[pltpu.VMEM((width, depth), bf16)],
        cost_estimate=pl.CostEstimate(
            flops=2 * n_cols * depth * width,
            bytes_accessed=2 * n_cols * depth,
            transcendentals=0,
        ),
    )(payoff, block)


def body(payoff, opp_strategy, opp_combos, seq_payoff, seq_parent):
    rows, width = opp_strategy.shape
    n_chip = lax.axis_size(CHIPS)
    n_y, n_seq = lax.axis_size("primal"), lax.axis_size("seq")
    core, seq = lax.axis_index("core"), lax.axis_index("seq")
    part_rows = rows // n_seq
    n_all = n_seq * width
    whole_payoff = lax.all_gather(seq_payoff, "seq", axis=1, tiled=True)
    same = (seq_parent[:, None] == seq_parent[None, :]).astype(bf16)

    scaled = (opp_combos.astype(f32)[:, None] * opp_strategy).astype(bf16)
    scaled = spread(scaled, n_chip, CHIPS).reshape(n_chip, rows, width)
    other = lax.ppermute(scaled, "core", SWAP)
    block = jnp.stack(
        [jnp.where(core == 0, scaled, other), jnp.where(core == 0, other, scaled)],
        axis=1,
    ).reshape(-1, width)

    inner = player_product(payoff, block).reshape(n_y * n_seq, part_rows, width)
    inner = exchange(inner, PLANE).reshape(n_y, n_seq, part_rows, width)
    inner = inner.astype(f32).sum(axis=0).astype(bf16)
    inner = jnp.swapaxes(inner, 0, 1).reshape(part_rows, n_all)
    gradient = lax.dot_general(
        inner, whole_payoff, (((1,), (1,)), ((), ())), preferred_element_type=f32
    )

    largest = jnp.max(jnp.abs(gradient), axis=1, keepdims=True)
    exponent = jnp.exp(-logit_span * gradient / (largest + epsilon))
    high = exponent.astype(bf16)
    low = (exponent - high.astype(f32)).astype(bf16)
    totals = jnp.dot(
        jnp.concatenate([high, low], axis=0), same, preferred_element_type=f32
    )
    strategy = exponent / (totals[:part_rows] + totals[part_rows:])
    through = jnp.dot(
        strategy.astype(bf16), whole_payoff, preferred_element_type=f32
    ).astype(bf16)

    through = jnp.swapaxes(through.reshape(part_rows, n_seq, width), 0, 1)
    through = jnp.broadcast_to(through[None], (n_y, *through.shape))
    player_block = exchange(through.reshape(n_y * n_seq, part_rows, width), PLANE)

    strategy = jnp.swapaxes(strategy.reshape(part_rows, n_seq, width), 0, 1)
    own_strategy = jnp.zeros((n_seq, part_rows, width), f32)
    for hop in range(n_seq):
        piece = pick(strategy, (seq + hop) % n_seq)
        if hop:
            piece = lax.ppermute(
                piece, "seq", [(i, (i + hop) % n_seq) for i in range(n_seq)]
            )
        own_strategy = lax.dynamic_update_index_in_dim(
            own_strategy, piece, (seq - hop) % n_seq, 0
        )
    own_strategy = own_strategy.reshape(rows, width)

    opp = opponent_product(payoff, player_block.reshape(-1, width), n_chip, rows)
    opp = pick(opp, core).astype(f32) + lax.ppermute(
        pick(opp, 1 - core), "core", SWAP
    ).astype(f32)
    opp = exchange(opp.astype(bf16), CHIPS)
    opp_grad = opp.astype(f32).sum(axis=0).T
    return own_strategy, opp_grad


def solution(mesh):
    n_dual, n_primal, n_seq = mesh.devices.shape
    fine = Mesh(
        mesh.devices.reshape(n_dual // 4, 2, 2, n_primal, n_seq),
        (*DUAL, *PLANE),
    )
    opponent_rows = ("primal", *DUAL)
    return jax.shard_map(
        body,
        mesh=fine,
        in_specs=(
            P(DUAL, "primal"),
            P(opponent_rows, "seq"),
            P(opponent_rows),
            P(None, "seq"),
            P(),
        ),
        out_specs=(P((*DUAL, "primal"), "seq"), P(opponent_rows, "seq")),
        check_vma=False,
    )
```

time: 148 us -> 163 us (1.10)
  the two profiles are of different devices: /device:TPU:1 before, /device:TPU:8 now
where the time goes in v2:
time: 163 us; the launch traced here: 162 us
  blocking collectives  67.6 us (41%)
  waiting for transfers between devices  31.7 us (19%)
  starting transfers between devices  25.5 us (16%)
  between operations  14.4 us (9%)
  Pallas kernels  10.2 us (6%)
  other arithmetic  5.15 us (3%)
  matrix products  3.91 us (2%)
  local copies, waits for them, and re-layouts  3.84 us (2%)
    all_to_all x2, blocking collectives, exchange(): return lax.all_to_all(blocks, axis, split_axis=0, concat_axis=0, tiled=True)  67.6 us
    all_to_all x2, waiting for transfers between devices, exchange(): return lax.all_to_all(blocks, axis, split_axis=0, concat_axis=0, tiled=True)  23.1 us
    all_to_all x2, starting transfers between devices, exchange(): return lax.all_to_all(blocks, axis, split_axis=0, concat_axis=0, tiled=True)  12.1 us
    ppermute x3, starting transfers between devices, body(): lax.ppermute(piece, 'seq', [(i, (i + hop) % n_seq) for i in range(n_seq)])  9.56 us
    pallas_call x1, Pallas kernels, opponent_product(): pl.pallas_call(opponent_kernel, grid=(chips // step,), in_specs=[pl.Block...  5.12 us
    pallas_call x1, Pallas kernels, player_product(): pl.pallas_call(player_kernel, grid=(n_rows // step,), in_specs=[pl.BlockS...  5.03 us
    ppermute x3, waiting for transfers between devices, body(): lax.ppermute(piece, 'seq', [(i, (i + hop) % n_seq) for i in range(n_seq)])  4.34 us
  transfers between devices with their start and end apart: 8, of which 6 were waited for; matrix products, arithmetic and copies ran while one was open for 2% of the time, Pallas kernels for 3%

profile of v2, /device:TPU:8, one launch (start us, length us, event | category | flops | bytes accessed | tf_op | source)
XLA Modules:
  0.0 162.2 jit_solution(7052935592376003345)
XLA Ops:
  7.2 0.0 all-gather.2.cloned.1.call-start
  7.2 0.7 all-gather.2.cloned.1.call-update
  7.9 0.7 convert_element_type.39
  8.6 1.0 multiply_convert_fusion
  9.6 26.7 %all_to_all.20 = bf16[8,128,256]{2,1,0:T(8,128)(2,1)S(1)} all-to-all(bf16[8,128,256]{2,1,0:T(8,128)(2,1)S(1)} %broadcast_in_dim.31), channel_id=1, replica_groups=mesh['x'=4,'zh'=2,'core'=2,'primal'=8,'seq'=4] {'x','zh'}, dimensions={0} | all-to-all | bytes 1048576 | tf_op jit(solution)/shard_map/all_to_all | solution.py:20
  36.3 1.9 %collective-permute-start = (bf16[8,128,256]{2,1,0:T(8,128)(2,1)S(1)}, bf16[8,128,256]{2,1,0:T(8,128)(2,1)S(1)}, u32[]{:S(2)}, u32[]{:S(2)}) collective-permute-start(bf16[8,128,256]{2,1,0:T(8,128)(2,1)S(1)} %all_to_all.20), channel_id=1, source_target_pairs={{0,32},{32,0},{1,33},{33,1},{2,34},{34,2},{3,35},{35,3},{4,36},{36... | collective-permute-start | bytes 1572872 | tf_op jit(solution)/shard_map/ppermute | solution.py:105
  38.2 1.9 %collective-permute-done = bf16[8,128,256]{2,1,0:T(8,128)(2,1)S(1)} collective-permute-done((bf16[8,128,256]{2,1,0:T(8,128)(2,1)S(1)}, bf16[8,128,256]{2,1,0:T(8,128)(2,1)S(1)}, u32[]{:S(2)}, u32[]{:S(2)}) %collective-permute-start) | collective-permute-done | bytes 524320 | tf_op jit(solution)/shard_map/ppermute | solution.py:105
  40.0 0.1 select_bitcast_fusion.1
  40.1 1.1 pad_maximum_fusion
  41.2 5.0 %shard_map.68 = bf16[1024,256]{1,0:T(8,128)(2,1)} custom-call(bf16[1024,2048]{1,0:T(8,128)(2,1)} %payoff_ref.3, bf16[2048,256]{1,0:T(8,128)(2,1)} %bitcast.42), custom_call_target="tpu_custom_call" | custom-call | flops 1073741824 | bytes 4194304 | tf_op jit(solution)/shard_map/pallas_call | solution.py:41
  46.2 0.0 copy-start.3
  46.2 40.9 %all_to_all.21 = bf16[32,32,256]{2,1,0:T(8,128)(2,1)S(1)} all-to-all(bf16[32,32,256]{2,1,0:T(8,128)(2,1)} %bitcast.45), channel_id=1, replica_groups=mesh['x'=4,'zh'=2,'core'=2,'primal'=8,'seq'=4] {'primal','seq'}, dimensions={0} | all-to-all | bytes 1048576 | tf_op jit(solution)/shard_map/all_to_all | solution.py:20
  87.2 0.1 reduce_sum.21
  87.3 0.0 all-gather.2.cloned.1.call-done
  87.3 0.0 copy-start
  87.3 2.6 %abs_reduce_fusion = (f32[32]{0:T(128)S(1)}, f32[32,1024]{1,0:T(8,128)S(1)}) fusion(bf16[32,1024]{1,0:T(8,128)(2,1)S(1)} %bitcast.47, bf16[1024,1024]{1,0:T(8,128)(2,1)} %all-gather.2.cloned.1.call-done), kind=kOutput, calls=%fused_computation.19 | convolution fusion | flops 67174368 | bytes 2293888 | tf_op jit(solution)/shard_map/dot_general | solution.py:115
  89.9 0.1 fusion.11
  90.0 0.0 copy-done.3
  90.0 0.9 fusion
  90.9 0.1 fusion.5
  91.0 0.0 copy-done
  91.0 0.5 convolution_convert_fusion
  91.5 0.8 broadcast_in_dim.35
  92.4 5.1 %all-to-all-start.2 = ((bf16[32,32,256]{2,1,0:T(8,128)(2,1)}), bf16[32,32,256]{2,1,0:T(8,128)(2,1)S(1)}, u32[]{:S(2)}, u32[]{:S(2)}) async-start(bf16[32,32,256]{2,1,0:T(8,128)(2,1)} %bitcast.12), calls=%async_computation.2 | async-start | bytes 1048576 | tf_op jit(solution)/shard_map/all_to_all | solution.py:20
  97.5 18.1 %all-to-all-done.2 = bf16[32,32,256]{2,1,0:T(8,128)(2,1)S(1)} async-done(((bf16[32,32,256]{2,1,0:T(8,128)(2,1)}), bf16[32,32,256]{2,1,0:T(8,128)(2,1)S(1)}, u32[]{:S(2)}, u32[]{:S(2)}) %all-to-all-start.2) | async-done | bytes 524320 | tf_op jit(solution)/shard_map/all_to_all | solution.py:20
  115.5 0.0 copy-start.1
  115.5 0.8 copy-done.1
  116.3 5.1 %shard_map.69 = bf16[2,8,256,128]{3,2,1,0:T(8,128)(2,1)} custom-call(bf16[1024,2048]{1,0:T(8,128)(2,1)} %payoff_ref.3, bf16[1024,256]{1,0:T(8,128)(2,1)} %bitcast.44), custom_call_target="tpu_custom_call" | custom-call | flops 1073741824 | bytes 4194304 | tf_op jit(solution)/shard_map/pallas_call | solution.py:75
  121.5 1.1 dynamic-slice_bitcast_fusion
  122.5 1.9 %collective-permute-start.4 = (bf16[8,256,128]{2,1,0:T(8,128)(2,1)S(1)}, bf16[8,256,128]{2,1,0:T(8,128)(2,1)S(1)}, u32[]{:S(2)}, u32[]{:S(2)}) collective-permute-start(bf16[8,256,128]{2,1,0:T(8,128)(2,1)S(1)} %dynamic-slice_bitcast_fusion), channel_id=1, source_target_pairs={{0,32},{32,0},{1,33},{33,1},{2,34},{34,2},{3,35},{35,3},{4,36},{36... | collective-permute-start | bytes 1572872 | tf_op jit(solution)/shard_map/ppermute | solution.py:149
  124.6 0.1 reshape.53
  124.7 1.7 %collective-permute-done.4 = bf16[8,256,128]{2,1,0:T(8,128)(2,1)S(1)} collective-permute-done((bf16[8,256,128]{2,1,0:T(8,128)(2,1)S(1)}, bf16[8,256,128]{2,1,0:T(8,128)(2,1)S(1)}, u32[]{:S(2)}, u32[]{:S(2)}) %collective-permute-start.4) | collective-permute-done | bytes 524320 | tf_op jit(solution)/shard_map/ppermute | solution.py:149
  126.3 2.0 %fusion.4 = bf16[8,256,128]{2,1,0:T(8,128)(2,1)} fusion(bf16[8,256,128]{2,1,0:T(8,128)(2,1)S(1)} %collective-permute-done.4, bf16[2,8,256,128]{3,2,1,0:T(8,128)(2,1)} %shard_map.69, s32[]{:T(128)S(6)} %select_n.93), kind=kLoop, calls=%fused_computation.7 | loop fusion | flops 1048576 | bytes 1572868 | tf_op jit(solution)/shard_map/convert_element_type | solution.py:152
  128.3 7.0 %all-to-all-start.3 = ((bf16[8,256,128]{2,1,0:T(8,128)(2,1)}), bf16[8,256,128]{2,1,0:T(8,128)(2,1)S(1)}, u32[]{:S(2)}, u32[]{:S(2)}) async-start(bf16[8,256,128]{2,1,0:T(8,128)(2,1)} %fusion.4), calls=%async_computation.3 | async-start | bytes 1048576 | tf_op jit(solution)/shard_map/all_to_all | solution.py:20
  135.4 0.1 constant_dynamic-slice_fusion
  135.5 1.9 %collective-permute-start.1 = (f32[32,256]{1,0:T(8,128)S(1)}, f32[32,256]{1,0:T(8,128)S(1)}, u32[]{:S(2)}, u32[]{:S(2)}) collective-permute-start(f32[32,256]{1,0:T(8,128)S(1)} %bitcast.53), channel_id=1, source_target_pairs={{0,1},{1,2},{2,3},{3,0},{4,5},{5,6},{6,7},{7,4},{8,9},{9,10},{10,1... | collective-permute-start | bytes 98312 | tf_op jit(solution)/shard_map/ppermute | solution.py:140
  137.4 3.9 %collective-permute-start.2 = (f32[32,256]{1,0:T(8,128)S(1)}, f32[32,256]{1,0:T(8,128)S(1)}, u32[]{:S(2)}, u32[]{:S(2)}) collective-permute-start(f32[32,256]{1,0:T(8,128)S(1)} %bitcast.52), channel_id=1, source_target_pairs={{0,2},{1,3},{2,0},{3,1},{4,6},{5,7},{6,4},{7,5},{8,10},{9,11},{10,... | collective-permute-start | bytes 98312 | tf_op jit(solution)/shard_map/ppermute | solution.py:140
  141.4 3.7 %collective-permute-start.3 = (f32[32,256]{1,0:T(8,128)S(1)}, f32[32,256]{1,0:T(8,128)S(1)}, u32[]{:S(2)}, u32[]{:S(2)}) collective-permute-start(f32[32,256]{1,0:T(8,128)S(1)} %bitcast.51), channel_id=1, source_target_pairs={{0,3},{1,0},{2,1},{3,2},{4,7},{5,4},{6,5},{7,6},{8,11},{9,8},{10,9... | collective-permute-start | bytes 98312 | tf_op jit(solution)/shard_map/ppermute | solution.py:140
  145.1 3.7 %collective-permute-done.1 = f32[32,256]{1,0:T(8,128)S(1)} collective-permute-done((f32[32,256]{1,0:T(8,128)S(1)}, f32[32,256]{1,0:T(8,128)S(1)}, u32[]{:S(2)}, u32[]{:S(2)}) %collective-permute-start.1) | collective-permute-done | bytes 32800 | tf_op jit(solution)/shard_map/ppermute | solution.py:140
  148.8 0.6 collective-permute-done.2
  149.5 0.0 collective-permute-done.3
  149.5 0.0 copy-start.2
  149.5 5.0 %all-to-all-done.3 = bf16[8,256,128]{2,1,0:T(8,128)(2,1)S(1)} async-done(((bf16[8,256,128]{2,1,0:T(8,128)(2,1)}), bf16[8,256,128]{2,1,0:T(8,128)(2,1)S(1)}, u32[]{:S(2)}, u32[]{:S(2)}) %all-to-all-start.3) | async-done | bytes 524320 | tf_op jit(solution)/shard_map/all_to_all | solution.py:20
  154.6 0.1 convert_reduce_fusion
  154.6 0.8 copy.14
  155.4 0.0 copy-done.2
  (13 shorter events, 0.1 us)
Async XLA Ops:
  7.2 80.1 %all-gather.2.cloned.1.call-start = ((), (), s32[]{:S(2)}) async-start(), calls=%async_computation.4 | async-start | bytes 2621440 | tf_op jit(solution)/shard_map/all_gather | solution.py:100
  36.3 3.8 %collective-permute-start = (bf16[8,128,256]{2,1,0:T(8,128)(2,1)S(1)}, bf16[8,128,256]{2,1,0:T(8,128)(2,1)S(1)}, u32[]{:S(2)}, u32[]{:S(2)}) collective-permute-start(bf16[8,128,256]{2,1,0:T(8,128)(2,1)S(1)} %all_to_all.20), channel_id=1, source_target_pairs={{0,32},{32,0},{1,33},{33,1},{2,34},{34,2},{3,35},{35,3},{4,36},{36... | collective-permute-start | bytes 1572872 | tf_op jit(solution)/shard_map/ppermute | solution.py:105
  46.2 43.8 %copy-start.3 = (s32[1024]{0:T(1024)S(1)}, s32[1024]{0:T(1024)}, u32[]{:S(2)}) copy-start(s32[1024]{0:T(1024)} %param.9) | copy-start | bytes 12292
  87.3 3.7 %copy-start = (bf16[1024,1024]{1,0:T(8,128)(2,1)S(1)}, bf16[1024,1024]{1,0:T(8,128)(2,1)}, u32[]{:S(2)}) copy-start(bf16[1024,1024]{1,0:T(8,128)(2,1)} %all-gather.2.cloned.1.call-done) | copy-start | bytes 6291460
  92.4 23.1 %all-to-all-start.2 = ((bf16[32,32,256]{2,1,0:T(8,128)(2,1)}), bf16[32,32,256]{2,1,0:T(8,128)(2,1)S(1)}, u32[]{:S(2)}, u32[]{:S(2)}) async-start(bf16[32,32,256]{2,1,0:T(8,128)(2,1)} %bitcast.12), calls=%async_computation.2 | async-start | bytes 1048576 | tf_op jit(solution)/shard_map/all_to_all | solution.py:20
  115.5 0.8 copy-start.1
  122.5 3.8 %collective-permute-start.4 = (bf16[8,256,128]{2,1,0:T(8,128)(2,1)S(1)}, bf16[8,256,128]{2,1,0:T(8,128)(2,1)S(1)}, u32[]{:S(2)}, u32[]{:S(2)}) collective-permute-start(bf16[8,256,128]{2,1,0:T(8,128)(2,1)S(1)} %dynamic-slice_bitcast_fusion), channel_id=1, source_target_pairs={{0,32},{32,0},{1,33},{33,1},{2,34},{34,2},{3,35},{35,3},{4,36},{36... | collective-permute-start | bytes 1572872 | tf_op jit(solution)/shard_map/ppermute | solution.py:149
  128.3 26.2 %all-to-all-start.3 = ((bf16[8,256,128]{2,1,0:T(8,128)(2,1)}), bf16[8,256,128]{2,1,0:T(8,128)(2,1)S(1)}, u32[]{:S(2)}, u32[]{:S(2)}) async-start(bf16[8,256,128]{2,1,0:T(8,128)(2,1)} %fusion.4), calls=%async_computation.3 | async-start | bytes 1048576 | tf_op jit(solution)/shard_map/all_to_all | solution.py:20
  135.5 13.3 %collective-permute-start.1 = (f32[32,256]{1,0:T(8,128)S(1)}, f32[32,256]{1,0:T(8,128)S(1)}, u32[]{:S(2)}, u32[]{:S(2)}) collective-permute-start(f32[32,256]{1,0:T(8,128)S(1)} %bitcast.53), channel_id=1, source_target_pairs={{0,1},{1,2},{2,3},{3,0},{4,5},{5,6},{6,7},{7,4},{8,9},{9,10},{10,1... | collective-permute-start | bytes 98312 | tf_op jit(solution)/shard_map/ppermute | solution.py:140
  137.4 12.1 %collective-permute-start.2 = (f32[32,256]{1,0:T(8,128)S(1)}, f32[32,256]{1,0:T(8,128)S(1)}, u32[]{:S(2)}, u32[]{:S(2)}) collective-permute-start(f32[32,256]{1,0:T(8,128)S(1)} %bitcast.52), channel_id=1, source_target_pairs={{0,2},{1,3},{2,0},{3,1},{4,6},{5,7},{6,4},{7,5},{8,10},{9,11},{10,... | collective-permute-start | bytes 98312 | tf_op jit(solution)/shard_map/ppermute | solution.py:140
  141.4 8.1 %collective-permute-start.3 = (f32[32,256]{1,0:T(8,128)S(1)}, f32[32,256]{1,0:T(8,128)S(1)}, u32[]{:S(2)}, u32[]{:S(2)}) collective-permute-start(f32[32,256]{1,0:T(8,128)S(1)} %bitcast.51), channel_id=1, source_target_pairs={{0,3},{1,0},{2,1},{3,2},{4,7},{5,4},{6,5},{7,6},{8,11},{9,8},{10,9... | collective-permute-start | bytes 98312 | tf_op jit(solution)/shard_map/ppermute | solution.py:140
  149.5 5.9 %copy-start.2 = (f32[4,32,256]{2,1,0:T(8,128)}, f32[4,32,256]{2,1,0:T(8,128)S(1)}, u32[]{:S(2)}) copy-start(f32[4,32,256]{2,1,0:T(8,128)S(1)} %bitcast_dynamic-update-slice_fusion.1) | copy-start | bytes 393220
Sparse Core Ops, SparseCore 0:
  10.1 62.5 all-gather.1

commit v3 on v1

v3 whole, which is shorter than its diff:
```python
import jax
import jax.numpy as jnp
from jax import lax
from jax.sharding import Mesh, PartitionSpec as P

logit_span = 6.0
epsilon = 1e-06

bf16 = jnp.bfloat16
f32 = jnp.float32
DUAL = ("x", "zh", "core")
PLANE = ("primal", "seq")
LINE = ("zh", "seq")
SWAP = ((0, 1), (1, 0))


def exchange(blocks, axis):
    return lax.all_to_all(blocks, axis, split_axis=0, concat_axis=0, tiled=True)


def spread(block, copies, axis):
    return exchange(jnp.broadcast_to(block[None], (copies, *block.shape)), axis)


def swap(block, axis):
    return lax.ppermute(block, axis, SWAP)


def shift(block, axis, hop):
    size = lax.axis_size(axis)
    return lax.ppermute(block, axis, [(i, (i + hop) % size) for i in range(size)])


def pick(stack, index):
    return lax.dynamic_index_in_dim(stack, index, 0, keepdims=False)


def in_order(first, own, other, axis):
    return jnp.stack(
        [jnp.where(first, own, other), jnp.where(first, other, own)], axis=axis
    )


def body(payoff, opp_strategy, opp_combos, seq_payoff, seq_parent):
    rows, width = opp_strategy.shape
    n_x, n_y, n_seq = (lax.axis_size(a) for a in ("x", "primal", "seq"))
    zh, core, seq = (lax.axis_index(a) for a in ("zh", "core", "seq"))
    part_rows = rows // n_seq
    n_all = n_seq * width
    half = n_all // 2
    same = (seq_parent[:, None] == seq_parent[None, :]).astype(bf16)

    scaled = (opp_combos.astype(f32)[:, None] * opp_strategy).astype(bf16)
    far = swap(scaled, "zh")
    near = spread(scaled, n_x, "x").reshape(n_x, rows, width)
    near_other = swap(near, "core")

    own_half = lax.dynamic_slice_in_dim(seq_payoff, core * half, half, 0)
    quarter = half // 2
    behind = shift(own_half, LINE, 1)
    ahead = shift(own_half, LINE, -1)
    across = jnp.concatenate(
        [shift(own_half[:quarter], LINE, 2), shift(own_half[quarter:], LINE, -2)],
        axis=0,
    )

    far = spread(far, n_x, "x").reshape(n_x, rows, width)
    far, ahead, across, behind = lax.optimization_barrier((far, ahead, across, behind))
    far_other = swap(far, "core")
    near = in_order(core == 0, near, near_other, 1)
    far = in_order(core == 0, far, far_other, 1)
    block = in_order(zh == 0, near, far, 1).reshape(-1, width)

    fetched = jnp.stack([ahead, across, behind])
    fetched_other = swap(fetched, "core")
    fetched = in_order(core == 0, fetched, fetched_other, 1).reshape(-1, n_all, width)
    whole = jnp.concatenate([seq_payoff[None], fetched], axis=0)

    inner = jnp.dot(payoff, block, preferred_element_type=f32).astype(bf16)
    inner = exchange(inner.reshape(n_y * n_seq, part_rows, width), PLANE)
    inner = inner.reshape(n_y, n_seq, part_rows, width).astype(f32).sum(axis=0)
    inner = inner.astype(bf16)
    gradient = sum(
        lax.dot_general(
            pick(inner, (seq + hop) % n_seq),
            whole[hop],
            (((1,), (1,)), ((), ())),
            preferred_element_type=f32,
        )
        for hop in range(n_seq)
    )

    largest = jnp.max(jnp.abs(gradient), axis=1, keepdims=True)
    exponent = jnp.exp(-logit_span * gradient / (largest + epsilon))
    high = exponent.astype(bf16)
    low = (exponent - high.astype(f32)).astype(bf16)
    totals = jnp.dot(
        jnp.concatenate([high, low], axis=0), same, preferred_element_type=f32
    )
    strategy = exponent / (totals[:part_rows] + totals[part_rows:])
    strategy_low = strategy.astype(bf16)
    through = jnp.stack(
        [
            jnp.dot(strategy_low, whole[hop], preferred_element_type=f32).astype(bf16)
            for hop in range(n_seq)
        ]
    )
    through = jnp.stack([pick(through, (i - seq) % n_seq) for i in range(n_seq)])
    through = jnp.broadcast_to(through[None], (n_y, *through.shape))
    player_block = exchange(through.reshape(n_y * n_seq, part_rows, width), PLANE)

    strategy = jnp.stack(jnp.split(strategy, n_seq, axis=1))
    own_strategy = jnp.zeros((n_seq, part_rows, width), f32)
    for hop in range(n_seq):
        piece = pick(strategy, (seq + hop) % n_seq)
        if hop:
            piece = shift(piece, "seq", hop)
        own_strategy = lax.dynamic_update_index_in_dim(
            own_strategy, piece, (seq - hop) % n_seq, 0
        )
    own_strategy, player_block = lax.optimization_barrier((own_strategy, player_block))
    own_strategy = own_strategy.reshape(rows, width)

    opp = lax.dot_general(
        player_block.reshape(-1, width),
        payoff,
        (((0,), (0,)), ((), ())),
        preferred_element_type=f32,
    ).astype(bf16)
    opp = opp.reshape(width, n_x, 2, 2, rows).transpose(2, 3, 1, 0, 4)

    def over_cores(pair):
        return (
            pick(pair, core).astype(f32)
            + swap(pick(pair, 1 - core), "core").astype(f32)
        ).astype(bf16)

    far = exchange(over_cores(pick(opp, 1 - zh)), "x")
    near = over_cores(pick(opp, zh))
    far, near = lax.optimization_barrier((far, near))
    far = swap(far.astype(f32).sum(axis=0).astype(bf16), "zh")
    near = exchange(near, "x").astype(f32).sum(axis=0)
    return own_strategy, (near + far.astype(f32)).T


def solution(mesh):
    n_dual, n_primal, n_seq = mesh.devices.shape
    fine = Mesh(
        mesh.devices.reshape(n_dual // 4, 2, 2, n_primal, n_seq),
        (*DUAL, *PLANE),
    )
    opponent_rows = ("primal", *DUAL)
    return jax.shard_map(
        body,
        mesh=fine,
        in_specs=(
            P(DUAL, "primal"),
            P(opponent_rows, "seq"),
            P(opponent_rows),
            P(None, "seq"),
            P(),
        ),
        out_specs=(P((*DUAL, "primal"), "seq"), P(opponent_rows, "seq")),
        check_vma=False,
    )
```

time: 148 us -> 148 us (level)
  blocking collectives: 71.6 us -> 0 us
  starting transfers between devices: 21.7 us -> 85.9 us
  waiting for transfers between devices: 31.7 us -> 37.7 us
    all_to_all x4 -> x0, blocking collectives: 71.6 us -> none  [exchange(): return lax.all_to_all(blocks, axis, split_axis=0, concat_axis=0, tiled=True)]
    ppermute x3 -> x14, starting transfers between devices: 14.8 us -> 53.2 us  [the longest x7 31.5 us: swap(): return lax.ppermute(block, axis, SWAP)]
    all_to_all x2 -> x6, starting transfers between devices: 6.96 us -> 32.8 us  [exchange(): return lax.all_to_all(blocks, axis, split_axis=0, concat_axis=0, tiled=True)]
    ppermute x3 -> x14, waiting for transfers between devices: 7.8 us -> 11.7 us  [the longest x7 7.46 us: shift(): lax.ppermute(block, axis, [(i, (i + hop) % size) for i in range(size)])]
    unnamed x8 -> x11, local copies, waits for them, and re-layouts: 4.06 us -> 0.87 us
    another operation x1, local copies, waits for them, and re-layouts: 3.14 us -> 0.01 us  [body(): strategy = jnp.stack(jnp.split(strategy, n_seq, axis=1))]
    dynamic_slice x1 -> x3, local copies, waits for them, and re-layouts: 0.67 us -> 3.15 us  [the longest x2 2.19 us: pick(): return lax.dynamic_index_in_dim(stack, index, 0, keepdims=False)]
    all_to_all x2 -> x6, waiting for transfers between devices: 23.9 us -> 25.9 us  [exchange(): return lax.all_to_all(blocks, axis, split_axis=0, concat_axis=0, tiled=True)]
  transfers between devices with their start and end apart: 5 -> 20, of which waited for: 5 -> 6; matrix products, arithmetic and copies ran while one was open for 1% -> 6% of each run, Pallas kernels for 0% -> 0%
where the time goes in v3:
time: 148 us; the launch traced here: 146 us
  starting transfers between devices  85.9 us (58%)
  waiting for transfers between devices  37.7 us (25%)
  local copies, waits for them, and re-layouts  9.17 us (6%)
  matrix products  7.63 us (5%)
  other arithmetic  4.37 us (3%)
    all_to_all x6, starting transfers between devices, exchange(): return lax.all_to_all(blocks, axis, split_axis=0, concat_axis=0, tiled=True)  32.8 us
    ppermute x7, starting transfers between devices, swap(): return lax.ppermute(block, axis, SWAP)  31.5 us
    all_to_all x6, waiting for transfers between devices, exchange(): return lax.all_to_all(blocks, axis, split_axis=0, concat_axis=0, tiled=True)  25.9 us
    ppermute x7, starting transfers between devices, shift(): lax.ppermute(block, axis, [(i, (i + hop) % size) for i in range(size)])  21.7 us
    ppermute x7, waiting for transfers between devices, shift(): lax.ppermute(block, axis, [(i, (i + hop) % size) for i in range(size)])  7.46 us
    ppermute x7, waiting for transfers between devices, swap(): return lax.ppermute(block, axis, SWAP)  4.26 us
    dot_general x1, matrix products, body(): lax.dot_general(player_block.reshape(-1, width), payoff, (((0,), (0,)), (...  3.5 us
  transfers between devices with their start and end apart: 20, of which 6 were waited for; matrix products, arithmetic and copies ran while one was open for 6% of the time, Pallas kernels for 0%

profile of v3, /device:TPU:1, one launch (start us, length us, event | category | flops | bytes accessed | tf_op | source)
XLA Modules:
  0.0 146.1 jit_solution(7877448062883027639)
XLA Ops:
  0.6 0.7 convert_element_type.80
  1.3 1.0 multiply_convert_fusion
  2.3 11.5 %collective-permute-start.1 = (bf16[128,256]{1,0:T(8,128)(2,1)S(1)}, bf16[128,256]{1,0:T(8,128)(2,1)S(1)}, u32[]{:S(2)}, u32[]{:S(2)}) collective-permute-start(bf16[128,256]{1,0:T(8,128)(2,1)S(1)} %multiply_convert_fusion), channel_id=1, source_target_pairs={{0,64},{64,0},{1,65},{65,1},{2,66},{66,2},{3,67},{67,3},{4,68},{68... | collective-permute-start | bytes 196616 | tf_op jit(solution)/shard_map/ppermute | solution.py:26
  13.8 0.7 broadcast_in_dim.37
  14.5 4.0 %all-to-all-start = ((bf16[4,128,256]{2,1,0:T(8,128)(2,1)}), bf16[4,128,256]{2,1,0:T(8,128)(2,1)S(1)}, u32[]{:S(2)}, u32[]{:S(2)}) async-start(bf16[4,128,256]{2,1,0:T(8,128)(2,1)} %broadcast_in_dim.37), calls=%async_computation | async-start | bytes 524288 | tf_op jit(solution)/shard_map/all_to_all | solution.py:18
  18.5 1.0 constant_dynamic-slice_fusion.10
  19.5 2.0 %collective-permute-start.2 = (bf16[512,256]{1,0:T(8,128)(2,1)S(1)}, bf16[512,256]{1,0:T(8,128)(2,1)S(1)}, u32[]{:S(2)}, u32[]{:S(2)}) collective-permute-start(bf16[512,256]{1,0:T(8,128)(2,1)S(1)} %constant_dynamic-slice_fusion.10), channel_id=1, source_target_pairs={{0,67},{1,0},{2,1},{3,2},{64,3},{65,64},{66,65},{67,66},{4,71},{5,... | collective-permute-start | bytes 786440 | tf_op jit(solution)/shard_map/ppermute | solution.py:31
  21.4 3.3 %collective-permute-start.5 = (bf16[512,256]{1,0:T(8,128)(2,1)S(1)}, bf16[512,256]{1,0:T(8,128)(2,1)S(1)}, u32[]{:S(2)}, u32[]{:S(2)}) collective-permute-start(bf16[512,256]{1,0:T(8,128)(2,1)S(1)} %constant_dynamic-slice_fusion.10), channel_id=1, source_target_pairs={{0,1},{1,2},{2,3},{3,64},{64,65},{65,66},{66,67},{67,0},{4,5},{5,6... | collective-permute-start | bytes 786440 | tf_op jit(solution)/shard_map/ppermute | solution.py:31
  24.8 1.0 constant_dynamic-slice_fusion
  25.8 1.9 %collective-permute-start.4 = (bf16[256,256]{1,0:T(8,128)(2,1)S(1)}, bf16[256,256]{1,0:T(8,128)(2,1)S(1)}, u32[]{:S(2)}, u32[]{:S(2)}) collective-permute-start(bf16[256,256]{1,0:T(8,128)(2,1)S(1)} %get-tuple-element.36), channel_id=1, source_target_pairs={{0,66},{1,67},{2,0},{3,1},{64,2},{65,3},{66,64},{67,65},{4,70},{5,... | collective-permute-start | bytes 393224 | tf_op jit(solution)/shard_map/ppermute | solution.py:31
  27.7 4.2 %collective-permute-start.3 = (bf16[256,256]{1,0:T(8,128)(2,1)S(1)}, bf16[256,256]{1,0:T(8,128)(2,1)S(1)}, u32[]{:S(2)}, u32[]{:S(2)}) collective-permute-start(bf16[256,256]{1,0:T(8,128)(2,1)S(1)} %get-tuple-element.35), channel_id=1, source_target_pairs={{0,2},{1,3},{2,64},{3,65},{64,66},{65,67},{66,0},{67,1},{4,6},{5,7... | collective-permute-start | bytes 393224 | tf_op jit(solution)/shard_map/ppermute | solution.py:31
  32.0 0.7 broadcast_in_dim.38
  32.7 4.2 %all-to-all-start.1 = ((bf16[4,128,256]{2,1,0:T(8,128)(2,1)}), bf16[4,128,256]{2,1,0:T(8,128)(2,1)S(1)}, u32[]{:S(2)}, u32[]{:S(2)}) async-start(bf16[4,128,256]{2,1,0:T(8,128)(2,1)} %broadcast_in_dim.38), calls=%async_computation.1 | async-start | bytes 524288 | tf_op jit(solution)/shard_map/all_to_all | solution.py:18
  36.9 4.8 %collective-permute-start = (bf16[4,128,256]{2,1,0:T(8,128)(2,1)S(1)}, bf16[4,128,256]{2,1,0:T(8,128)(2,1)S(1)}, u32[]{:S(2)}, u32[]{:S(2)}) collective-permute-start(bf16[4,128,256]{2,1,0:T(8,128)(2,1)S(1)} %all-to-all-done), channel_id=1, source_target_pairs={{0,32},{32,0},{1,33},{33,1},{2,34},{34,2},{3,35},{35,3},{4,36},{36... | collective-permute-start | bytes 786440 | tf_op jit(solution)/shard_map/ppermute | solution.py:26
  41.8 0.6 all-to-all-done.1
  42.5 6.2 %collective-permute-start.6 = (bf16[4,128,256]{2,1,0:T(8,128)(2,1)S(1)}, bf16[4,128,256]{2,1,0:T(8,128)(2,1)S(1)}, u32[]{:S(2)}, u32[]{:S(2)}) collective-permute-start(bf16[4,128,256]{2,1,0:T(8,128)(2,1)S(1)} %all-to-all-done.1), channel_id=1, source_target_pairs={{0,32},{32,0},{1,33},{33,1},{2,34},{34,2},{3,35},{35,3},{4,36},{36... | collective-permute-start | bytes 786440 | tf_op jit(solution)/shard_map/ppermute | solution.py:26
  48.8 1.9 %collective-permute-start.7 = (bf16[3,512,256]{2,1,0:T(8,128)(2,1)S(1)}, bf16[3,512,256]{2,1,0:T(8,128)(2,1)S(1)}, u32[]{:S(2)}, u32[]{:S(2)}) collective-permute-start(bf16[3,512,256]{2,1,0:T(8,128)(2,1)S(1)} %pad_maximum_fusion.1), channel_id=1, source_target_pairs={{0,32},{32,0},{1,33},{33,1},{2,34},{34,2},{3,35},{35,3},{4,36},{36... | collective-permute-start | bytes 2359304 | tf_op jit(solution)/shard_map/ppermute | solution.py:26
  50.9 0.2 broadcast_select_fusion.1
  51.2 1.3 fusion.4
  52.5 1.0 copy.23
  53.5 12.5 %all-to-all-start.2 = ((bf16[32,32,256]{2,1,0:T(8,128)(2,1)}), bf16[32,32,256]{2,1,0:T(8,128)(2,1)S(1)}, u32[]{:S(2)}, u32[]{:S(2)}) async-start(bf16[32,32,256]{2,1,0:T(8,128)(2,1)} %bitcast.7), calls=%async_computation.2 | async-start | bytes 1048576 | tf_op jit(solution)/shard_map/all_to_all | solution.py:18
  66.5 16.6 %all-to-all-done.2 = bf16[32,32,256]{2,1,0:T(8,128)(2,1)S(1)} async-done(((bf16[32,32,256]{2,1,0:T(8,128)(2,1)}), bf16[32,32,256]{2,1,0:T(8,128)(2,1)S(1)}, u32[]{:S(2)}, u32[]{:S(2)}) %all-to-all-start.2) | async-done | bytes 524320 | tf_op jit(solution)/shard_map/all_to_all | solution.py:18
  83.2 0.2 fusion.20
  83.4 0.3 convolution_add_fusion.2
  83.7 0.3 convolution_add_fusion.1
  83.9 0.4 abs_reduce_fusion
  84.5 0.9 fusion
  85.6 0.2 fusion.7
  86.3 0.9 broadcast_in_dim.42
  87.2 5.2 %all-to-all-start.3 = ((bf16[32,32,256]{2,1,0:T(8,128)(2,1)}), bf16[32,32,256]{2,1,0:T(8,128)(2,1)S(1)}, u32[]{:S(2)}, u32[]{:S(2)}) async-start(bf16[32,32,256]{2,1,0:T(8,128)(2,1)} %bitcast.35), calls=%async_computation.3 | async-start | bytes 1048576 | tf_op jit(solution)/shard_map/all_to_all | solution.py:18
  92.5 3.1 %collective-permute-start.8 = (f32[32,256]{1,0:T(8,128)S(1)}, f32[32,256]{1,0:T(8,128)S(1)}, u32[]{:S(2)}, u32[]{:S(2)}) collective-permute-start(f32[32,256]{1,0:T(8,128)S(1)} %get-tuple-element.43), channel_id=1, source_target_pairs={{0,1},{1,2},{2,3},{3,0},{4,5},{5,6},{6,7},{7,4},{8,9},{9,10},{10,1... | collective-permute-start | bytes 98312 | tf_op jit(solution)/shard_map/ppermute | solution.py:31
  95.7 4.0 %collective-permute-start.9 = (f32[32,256]{1,0:T(8,128)S(1)}, f32[32,256]{1,0:T(8,128)S(1)}, u32[]{:S(2)}, u32[]{:S(2)}) collective-permute-start(f32[32,256]{1,0:T(8,128)S(1)} %get-tuple-element.42), channel_id=1, source_target_pairs={{0,2},{1,3},{2,0},{3,1},{4,6},{5,7},{6,4},{7,5},{8,10},{9,11},{10,... | collective-permute-start | bytes 98312 | tf_op jit(solution)/shard_map/ppermute | solution.py:31
  99.7 3.1 %collective-permute-start.10 = (f32[32,256]{1,0:T(8,128)S(1)}, f32[32,256]{1,0:T(8,128)S(1)}, u32[]{:S(2)}, u32[]{:S(2)}) collective-permute-start(f32[32,256]{1,0:T(8,128)S(1)} %get-tuple-element.41), channel_id=1, source_target_pairs={{0,3},{1,0},{2,1},{3,2},{4,7},{5,4},{6,5},{7,6},{8,11},{9,8},{10,9... | collective-permute-start | bytes 98312 | tf_op jit(solution)/shard_map/ppermute | solution.py:31
  102.8 7.4 %collective-permute-done.9 = f32[32,256]{1,0:T(8,128)S(1)} collective-permute-done((f32[32,256]{1,0:T(8,128)S(1)}, f32[32,256]{1,0:T(8,128)S(1)}, u32[]{:S(2)}, u32[]{:S(2)}) %collective-permute-start.9) | collective-permute-done | bytes 32800 | tf_op jit(solution)/shard_map/ppermute | solution.py:31
  110.3 3.5 %convolution_convert_fusion = bf16[256,2048]{1,0:T(8,128)(2,1)S(1)} fusion(bf16[1024,256]{1,0:T(8,128)(2,1)S(1)} %bitcast.124, bf16[1024,2048]{1,0:T(8,128)(2,1)} %param.5), kind=kOutput, calls=%fused_computation.2 | convolution fusion | flops 1074266112 | bytes 5767168 | tf_op jit(solution)/shard_map/dot_general | solution.py:124
  113.8 0.8 reshape.178
  114.6 2.2 %constant_dynamic-slice_fusion.2 = (bf16[256,4,1,1,128]{4,3,2,1,0:T(2,128)(2,1)S(1)}, bf16[256,4,1,1,128]{4,3,2,1,0:T(2,128)(2,1)S(1)}, bf16[256,4,1,1,128]{4,3,...) fusion(bf16[256,4,2,2,128]{4,3,2,1,0:T(2,128)(2,1)S(1)} %reshape.178, s32[]{:T(128)S(6)} %select_n.224, s32[]{:T(128)S(6)} %select_n.220, ...), kind=kLoop, calls=%fused_computation.80 | loop fusion | bytes 2097168 | tf_op jit(solution)/shard_map/jit(dynamic_index_in_dim)/dynamic_slice | solution.py:35
  116.9 3.2 %collective-permute-start.11 = (bf16[4,256,128]{2,1,0:T(8,128)(2,1)S(1)}, bf16[4,256,128]{2,1,0:T(8,128)(2,1)S(1)}, u32[]{:S(2)}, u32[]{:S(2)}) collective-permute-start(bf16[4,256,128]{2,1,0:T(8,128)(2,1)S(1)} %bitcast.126), channel_id=1, source_target_pairs={{0,32},{32,0},{1,33},{33,1},{2,34},{34,2},{3,35},{35,3},{4,36},{36... | collective-permute-start | bytes 786440 | tf_op jit(solution)/shard_map/ppermute | solution.py:26
  120.1 1.9 %collective-permute-start.12 = (bf16[4,256,128]{2,1,0:T(8,128)(2,1)S(1)}, bf16[4,256,128]{2,1,0:T(8,128)(2,1)S(1)}, u32[]{:S(2)}, u32[]{:S(2)}) collective-permute-start(bf16[4,256,128]{2,1,0:T(8,128)(2,1)S(1)} %bitcast.125), channel_id=1, source_target_pairs={{0,32},{32,0},{1,33},{33,1},{2,34},{34,2},{3,35},{35,3},{4,36},{36... | collective-permute-start | bytes 786440 | tf_op jit(solution)/shard_map/ppermute | solution.py:26
  122.1 0.8 fusion.12
  122.8 3.4 %all-to-all-start.4 = ((bf16[4,256,128]{2,1,0:T(8,128)(2,1)}), bf16[4,256,128]{2,1,0:T(8,128)(2,1)S(1)}, u32[]{:S(2)}, u32[]{:S(2)}) async-start(bf16[4,256,128]{2,1,0:T(8,128)(2,1)} %fusion.12), calls=%async_computation.4 | async-start | bytes 524288 | tf_op jit(solution)/shard_map/all_to_all | solution.py:18
  126.2 0.8 fusion.11
  127.0 5.2 %all-to-all-done.4 = bf16[4,256,128]{2,1,0:T(8,128)(2,1)S(1)} async-done(((bf16[4,256,128]{2,1,0:T(8,128)(2,1)}), bf16[4,256,128]{2,1,0:T(8,128)(2,1)S(1)}, u32[]{:S(2)}, u32[]{:S(2)}) %all-to-all-start.4) | async-done | bytes 262176 | tf_op jit(solution)/shard_map/all_to_all | solution.py:18
  132.2 3.4 %all-to-all-start.5 = ((bf16[4,256,128]{2,1,0:T(8,128)(2,1)}), bf16[4,256,128]{2,1,0:T(8,128)(2,1)S(1)}, u32[]{:S(2)}, u32[]{:S(2)}) async-start(bf16[4,256,128]{2,1,0:T(8,128)(2,1)} %fusion.11), calls=%async_computation.5 | async-start | bytes 524288 | tf_op jit(solution)/shard_map/all_to_all | solution.py:18
  135.6 1.9 %collective-permute-start.13 = (bf16[256,128]{1,0:T(8,128)(2,1)S(1)}, bf16[256,128]{1,0:T(8,128)(2,1)S(1)}, u32[]{:S(2)}, u32[]{:S(2)}) collective-permute-start(bf16[256,128]{1,0:T(8,128)(2,1)S(1)} %reduce_sum.35), channel_id=1, source_target_pairs={{0,64},{64,0},{1,65},{65,1},{2,66},{66,2},{3,67},{67,3},{4,68},{68... | collective-permute-start | bytes 196616 | tf_op jit(solution)/shard_map/ppermute | solution.py:26
  137.6 3.5 %all-to-all-done.5 = bf16[4,256,128]{2,1,0:T(8,128)(2,1)S(1)} async-done(((bf16[4,256,128]{2,1,0:T(8,128)(2,1)}), bf16[4,256,128]{2,1,0:T(8,128)(2,1)S(1)}, u32[]{:S(2)}, u32[]{:S(2)}) %all-to-all-start.5) | async-done | bytes 262176 | tf_op jit(solution)/shard_map/all_to_all | solution.py:18
  141.1 4.2 %collective-permute-done.13 = bf16[256,128]{1,0:T(8,128)(2,1)S(1)} collective-permute-done((bf16[256,128]{1,0:T(8,128)(2,1)S(1)}, bf16[256,128]{1,0:T(8,128)(2,1)S(1)}, u32[]{:S(2)}, u32[]{:S(2)}) %collective-permute-start.13) | collective-permute-done | bytes 65568 | tf_op jit(solution)/shard_map/ppermute | solution.py:26
  145.4 0.8 copy.28
  (51 shorter events, 1.8 us)
Async XLA Ops:
  2.3 29.7 %collective-permute-start.1 = (bf16[128,256]{1,0:T(8,128)(2,1)S(1)}, bf16[128,256]{1,0:T(8,128)(2,1)S(1)}, u32[]{:S(2)}, u32[]{:S(2)}) collective-permute-start(bf16[128,256]{1,0:T(8,128)(2,1)S(1)} %multiply_convert_fusion), channel_id=1, source_target_pairs={{0,64},{64,0},{1,65},{65,1},{2,66},{66,2},{3,67},{67,3},{4,68},{68... | collective-permute-start | bytes 196616 | tf_op jit(solution)/shard_map/ppermute | solution.py:26
  14.5 17.5 %all-to-all-start = ((bf16[4,128,256]{2,1,0:T(8,128)(2,1)}), bf16[4,128,256]{2,1,0:T(8,128)(2,1)S(1)}, u32[]{:S(2)}, u32[]{:S(2)}) async-start(bf16[4,128,256]{2,1,0:T(8,128)(2,1)} %broadcast_in_dim.37), calls=%async_computation | async-start | bytes 524288 | tf_op jit(solution)/shard_map/all_to_all | solution.py:18
  19.5 23.0 %collective-permute-start.2 = (bf16[512,256]{1,0:T(8,128)(2,1)S(1)}, bf16[512,256]{1,0:T(8,128)(2,1)S(1)}, u32[]{:S(2)}, u32[]{:S(2)}) collective-permute-start(bf16[512,256]{1,0:T(8,128)(2,1)S(1)} %constant_dynamic-slice_fusion.10), channel_id=1, source_target_pairs={{0,67},{1,0},{2,1},{3,2},{64,3},{65,64},{66,65},{67,66},{4,71},{5,... | collective-permute-start | bytes 786440 | tf_op jit(solution)/shard_map/ppermute | solution.py:31
  21.4 21.1 %collective-permute-start.5 = (bf16[512,256]{1,0:T(8,128)(2,1)S(1)}, bf16[512,256]{1,0:T(8,128)(2,1)S(1)}, u32[]{:S(2)}, u32[]{:S(2)}) collective-permute-start(bf16[512,256]{1,0:T(8,128)(2,1)S(1)} %constant_dynamic-slice_fusion.10), channel_id=1, source_target_pairs={{0,1},{1,2},{2,3},{3,64},{64,65},{65,66},{66,67},{67,0},{4,5},{5,6... | collective-permute-start | bytes 786440 | tf_op jit(solution)/shard_map/ppermute | solution.py:31
  25.8 16.0 %collective-permute-start.4 = (bf16[256,256]{1,0:T(8,128)(2,1)S(1)}, bf16[256,256]{1,0:T(8,128)(2,1)S(1)}, u32[]{:S(2)}, u32[]{:S(2)}) collective-permute-start(bf16[256,256]{1,0:T(8,128)(2,1)S(1)} %get-tuple-element.36), channel_id=1, source_target_pairs={{0,66},{1,67},{2,0},{3,1},{64,2},{65,3},{66,64},{67,65},{4,70},{5,... | collective-permute-start | bytes 393224 | tf_op jit(solution)/shard_map/ppermute | solution.py:31
  27.7 14.1 %collective-permute-start.3 = (bf16[256,256]{1,0:T(8,128)(2,1)S(1)}, bf16[256,256]{1,0:T(8,128)(2,1)S(1)}, u32[]{:S(2)}, u32[]{:S(2)}) collective-permute-start(bf16[256,256]{1,0:T(8,128)(2,1)S(1)} %get-tuple-element.35), channel_id=1, source_target_pairs={{0,2},{1,3},{2,64},{3,65},{64,66},{65,67},{66,0},{67,1},{4,6},{5,7... | collective-permute-start | bytes 393224 | tf_op jit(solution)/shard_map/ppermute | solution.py:31
  32.7 9.8 %all-to-all-start.1 = ((bf16[4,128,256]{2,1,0:T(8,128)(2,1)}), bf16[4,128,256]{2,1,0:T(8,128)(2,1)S(1)}, u32[]{:S(2)}, u32[]{:S(2)}) async-start(bf16[4,128,256]{2,1,0:T(8,128)(2,1)} %broadcast_in_dim.38), calls=%async_computation.1 | async-start | bytes 524288 | tf_op jit(solution)/shard_map/all_to_all | solution.py:18
  36.9 13.8 %collective-permute-start = (bf16[4,128,256]{2,1,0:T(8,128)(2,1)S(1)}, bf16[4,128,256]{2,1,0:T(8,128)(2,1)S(1)}, u32[]{:S(2)}, u32[]{:S(2)}) collective-permute-start(bf16[4,128,256]{2,1,0:T(8,128)(2,1)S(1)} %all-to-all-done), channel_id=1, source_target_pairs={{0,32},{32,0},{1,33},{33,1},{2,34},{34,2},{3,35},{35,3},{4,36},{36... | collective-permute-start | bytes 786440 | tf_op jit(solution)/shard_map/ppermute | solution.py:26
  42.5 8.7 %copy-start.2 = (bf16[1024,2048]{1,0:T(8,128)(2,1)S(1)}, bf16[1024,2048]{1,0:T(8,128)(2,1)}, u32[]{:S(2)}) copy-start(bf16[1024,2048]{1,0:T(8,128)(2,1)} %param.5) | copy-start | bytes 12582916
  42.5 8.3 %collective-permute-start.6 = (bf16[4,128,256]{2,1,0:T(8,128)(2,1)S(1)}, bf16[4,128,256]{2,1,0:T(8,128)(2,1)S(1)}, u32[]{:S(2)}, u32[]{:S(2)}) collective-permute-start(bf16[4,128,256]{2,1,0:T(8,128)(2,1)S(1)} %all-to-all-done.1), channel_id=1, source_target_pairs={{0,32},{32,0},{1,33},{33,1},{2,34},{34,2},{3,35},{35,3},{4,36},{36... | collective-permute-start | bytes 786440 | tf_op jit(solution)/shard_map/ppermute | solution.py:26
  48.8 17.4 %collective-permute-start.7 = (bf16[3,512,256]{2,1,0:T(8,128)(2,1)S(1)}, bf16[3,512,256]{2,1,0:T(8,128)(2,1)S(1)}, u32[]{:S(2)}, u32[]{:S(2)}) collective-permute-start(bf16[3,512,256]{2,1,0:T(8,128)(2,1)S(1)} %pad_maximum_fusion.1), channel_id=1, source_target_pairs={{0,32},{32,0},{1,33},{33,1},{2,34},{34,2},{3,35},{35,3},{4,36},{36... | collective-permute-start | bytes 2359304 | tf_op jit(solution)/shard_map/ppermute | solution.py:26
  53.5 29.6 %copy-start = (bf16[1024,256]{1,0:T(8,128)(2,1)S(1)}, bf16[1024,256]{1,0:T(8,128)(2,1)}, u32[]{:S(2)}) copy-start(bf16[1024,256]{1,0:T(8,128)(2,1)} %param.8) | copy-start | bytes 1572868
  53.5 29.5 %all-to-all-start.2 = ((bf16[32,32,256]{2,1,0:T(8,128)(2,1)}), bf16[32,32,256]{2,1,0:T(8,128)(2,1)S(1)}, u32[]{:S(2)}, u32[]{:S(2)}) async-start(bf16[32,32,256]{2,1,0:T(8,128)(2,1)} %bitcast.7), calls=%async_computation.2 | async-start | bytes 1048576 | tf_op jit(solution)/shard_map/all_to_all | solution.py:18
  66.3 18.1 %copy-start.3 = (s32[1024]{0:T(1024)S(1)}, s32[1024]{0:T(1024)}, u32[]{:S(2)}) copy-start(s32[1024]{0:T(1024)} %param.9) | copy-start | bytes 12292
  87.2 23.1 %all-to-all-start.3 = ((bf16[32,32,256]{2,1,0:T(8,128)(2,1)}), bf16[32,32,256]{2,1,0:T(8,128)(2,1)S(1)}, u32[]{:S(2)}, u32[]{:S(2)}) async-start(bf16[32,32,256]{2,1,0:T(8,128)(2,1)} %bitcast.35), calls=%async_computation.3 | async-start | bytes 1048576 | tf_op jit(solution)/shard_map/all_to_all | solution.py:18
  92.5 10.3 %collective-permute-start.8 = (f32[32,256]{1,0:T(8,128)S(1)}, f32[32,256]{1,0:T(8,128)S(1)}, u32[]{:S(2)}, u32[]{:S(2)}) collective-permute-start(f32[32,256]{1,0:T(8,128)S(1)} %get-tuple-element.43), channel_id=1, source_target_pairs={{0,1},{1,2},{2,3},{3,0},{4,5},{5,6},{6,7},{7,4},{8,9},{9,10},{10,1... | collective-permute-start | bytes 98312 | tf_op jit(solution)/shard_map/ppermute | solution.py:31
  95.7 14.6 %collective-permute-start.9 = (f32[32,256]{1,0:T(8,128)S(1)}, f32[32,256]{1,0:T(8,128)S(1)}, u32[]{:S(2)}, u32[]{:S(2)}) collective-permute-start(f32[32,256]{1,0:T(8,128)S(1)} %get-tuple-element.42), channel_id=1, source_target_pairs={{0,2},{1,3},{2,0},{3,1},{4,6},{5,7},{6,4},{7,5},{8,10},{9,11},{10,... | collective-permute-start | bytes 98312 | tf_op jit(solution)/shard_map/ppermute | solution.py:31
  99.7 10.6 %collective-permute-start.10 = (f32[32,256]{1,0:T(8,128)S(1)}, f32[32,256]{1,0:T(8,128)S(1)}, u32[]{:S(2)}, u32[]{:S(2)}) collective-permute-start(f32[32,256]{1,0:T(8,128)S(1)} %get-tuple-element.41), channel_id=1, source_target_pairs={{0,3},{1,0},{2,1},{3,2},{4,7},{5,4},{6,5},{7,6},{8,11},{9,8},{10,9... | collective-permute-start | bytes 98312 | tf_op jit(solution)/shard_map/ppermute | solution.py:31
  110.3 4.3 %copy-start.1 = (f32[4,32,256]{2,1,0:T(8,128)}, f32[4,32,256]{2,1,0:T(8,128)S(1)}, u32[]{:S(2)}) copy-start(f32[4,32,256]{2,1,0:T(8,128)S(1)} %bitcast_dynamic-update-slice_fusion) | copy-start | bytes 393220
  116.9 5.2 %collective-permute-start.11 = (bf16[4,256,128]{2,1,0:T(8,128)(2,1)S(1)}, bf16[4,256,128]{2,1,0:T(8,128)(2,1)S(1)}, u32[]{:S(2)}, u32[]{:S(2)}) collective-permute-start(bf16[4,256,128]{2,1,0:T(8,128)(2,1)S(1)} %bitcast.126), channel_id=1, source_target_pairs={{0,32},{32,0},{1,33},{33,1},{2,34},{34,2},{3,35},{35,3},{4,36},{36... | collective-permute-start | bytes 786440 | tf_op jit(solution)/shard_map/ppermute | solution.py:26
  120.1 6.1 %collective-permute-start.12 = (bf16[4,256,128]{2,1,0:T(8,128)(2,1)S(1)}, bf16[4,256,128]{2,1,0:T(8,128)(2,1)S(1)}, u32[]{:S(2)}, u32[]{:S(2)}) collective-permute-start(bf16[4,256,128]{2,1,0:T(8,128)(2,1)S(1)} %bitcast.125), channel_id=1, source_target_pairs={{0,32},{32,0},{1,33},{33,1},{2,34},{34,2},{3,35},{35,3},{4,36},{36... | collective-permute-start | bytes 786440 | tf_op jit(solution)/shard_map/ppermute | solution.py:26
  122.8 9.4 %all-to-all-start.4 = ((bf16[4,256,128]{2,1,0:T(8,128)(2,1)}), bf16[4,256,128]{2,1,0:T(8,128)(2,1)S(1)}, u32[]{:S(2)}, u32[]{:S(2)}) async-start(bf16[4,256,128]{2,1,0:T(8,128)(2,1)} %fusion.12), calls=%async_computation.4 | async-start | bytes 524288 | tf_op jit(solution)/shard_map/all_to_all | solution.py:18
  132.2 8.9 %all-to-all-start.5 = ((bf16[4,256,128]{2,1,0:T(8,128)(2,1)}), bf16[4,256,128]{2,1,0:T(8,128)(2,1)S(1)}, u32[]{:S(2)}, u32[]{:S(2)}) async-start(bf16[4,256,128]{2,1,0:T(8,128)(2,1)} %fusion.11), calls=%async_computation.5 | async-start | bytes 524288 | tf_op jit(solution)/shard_map/all_to_all | solution.py:18
  135.6 9.7 %collective-permute-start.13 = (bf16[256,128]{1,0:T(8,128)(2,1)S(1)}, bf16[256,128]{1,0:T(8,128)(2,1)S(1)}, u32[]{:S(2)}, u32[]{:S(2)}) collective-permute-start(bf16[256,128]{1,0:T(8,128)(2,1)S(1)} %reduce_sum.35), channel_id=1, source_target_pairs={{0,64},{64,0},{1,65},{65,1},{2,66},{66,2},{3,67},{67,3},{4,68},{68... | collective-permute-start | bytes 196616 | tf_op jit(solution)/shard_map/ppermute | solution.py:26

commit v4 on v1

--- a/solution.py
+++ b/solution.py
@@ -1,6 +1,8 @@
 import jax
 import jax.numpy as jnp
 from jax import lax
+from jax.experimental import pallas as pl
+from jax.experimental.pallas import tpu as pltpu
 from jax.sharding import Mesh, PartitionSpec as P
 
 logit_span = 6.0
@@ -9,6 +11,7 @@
 bf16 = jnp.bfloat16
 f32 = jnp.float32
 DUAL = ("x", "zh", "core")
+KERNEL_VMEM = 16 << 20
 SWAP = ((0, 1), (1, 0))
 
 
@@ -20,14 +23,83 @@
     return exchange(jnp.broadcast_to(block[None], (copies, *block.shape)), axis)
 
 
-def pick(pair, index):
-    return lax.dynamic_index_in_dim(pair, index, 0, keepdims=False)
+def pick(pair, first):
+    return jnp.where(first, pair[0], pair[1])
+
+
+def resident(array):
+    return pltpu.with_memory_space_constraint(array, pltpu.VMEM)
+
+
+VMEM_SPEC = pl.BlockSpec(memory_space=pltpu.VMEM)
+
+
+def player_kernel(payoff_ref, block_ref, out_ref):
+    step = 256
+
+    @pl.loop(0, payoff_ref.shape[0] // step)
+    def _(i):
+        at = pl.ds(pl.multiple_of(i * step, step), step)
+        out_ref[at, :] = jnp.dot(
+            payoff_ref[at, :], block_ref[...], preferred_element_type=f32
+        ).astype(bf16)
+
+
+def player_product(payoff, block):
+    n_rows, depth = payoff.shape
+    width = block.shape[1]
+    return pl.pallas_call(
+        player_kernel,
+        in_specs=[VMEM_SPEC] * 2,
+        out_specs=VMEM_SPEC,
+        out_shape=jax.ShapeDtypeStruct((n_rows, width), bf16),
+        compiler_params=pltpu.CompilerParams(vmem_limit_bytes=KERNEL_VMEM),
+        cost_estimate=pl.CostEstimate(
+            flops=2 * n_rows * depth * width,
+            bytes_accessed=2 * n_rows * depth,
+            transcendentals=0,
+        ),
+    )(resident(payoff), block)
+
+
+def opponent_kernel(payoff_ref, block_ref, out_ref, turned):
+    turned[...] = block_ref[...].T
+    chips, width, rows = out_ref.shape[1:]
+
+    @pl.loop(0, chips)
+    def _(chip):
+        at = pl.ds(pl.multiple_of(chip * 2 * rows, 2 * rows), 2 * rows)
+        total = jnp.dot(
+            turned[...], payoff_ref[:, at], preferred_element_type=f32
+        ).astype(bf16)
+        out_ref[0, chip] = total[:, :rows]
+        out_ref[1, chip] = total[:, rows:]
+
+
+def opponent_product(payoff, block, chips, rows):
+    depth, n_cols = payoff.shape
+    width = block.shape[1]
+    return pl.pallas_call(
+        opponent_kernel,
+        in_specs=[VMEM_SPEC] * 2,
+        out_specs=VMEM_SPEC,
+        out_shape=jax.ShapeDtypeStruct((2, chips, width, rows), bf16),
+        scratch_shapes=[pltpu.VMEM((width, depth), bf16)],
+        compiler_params=pltpu.CompilerParams(vmem_limit_bytes=KERNEL_VMEM),
+        cost_estimate=pl.CostEstimate(
+            flops=2 * n_cols * depth * width,
+            bytes_accessed=2 * n_cols * depth,
+            transcendentals=0,
+        ),
+    )(resident(payoff), block)
 
 
 def body(payoff, opp_strategy, opp_combos, seq_payoff, seq_parent):
     rows, width = opp_strategy.shape
     n_x, n_zh, n_y, n_seq = (lax.axis_size(a) for a in ("x", "zh", "primal", "seq"))
     core, zh, seq = (lax.axis_index(a) for a in ("core", "zh", "seq"))
+    core_first, zh_first = core == 0, zh == 0
+    core_second, zh_second = core == 1, zh == 1
     same = (seq_parent[:, None] == seq_parent[None, :]).astype(bf16)
 
     scaled = (opp_combos.astype(f32)[:, None] * opp_strategy).astype(bf16)
@@ -43,11 +115,18 @@
 
     mixed = spread(mixed, n_x, "x").reshape(n_x * n_zh, rows, width)
     other = lax.ppermute(mixed, "core", SWAP)
+
     block = jnp.stack(
-        [jnp.where(core == 0, mixed, other), jnp.where(core == 0, other, mixed)], axis=1
-    ).reshape(-1, width)
-
-    partial_grad = jnp.dot(payoff, block, preferred_element_type=f32).astype(bf16)
+        [jnp.where(core_first, mixed, other), jnp.where(core_first, other, mixed)],
+        axis=1,
+    )
+    partial_grad = player_product(payoff, block.reshape(-1, width))
+    own_at = (seq * width).astype(jnp.uint32)
+    partial_grad, own_at, core_first, core_second, zh_first, zh_second = (
+        lax.optimization_barrier(
+            (partial_grad, own_at, core_first, core_second, zh_first, zh_second)
+        )
+    )
     partial_grad = exchange(partial_grad.reshape(n_y, rows, width), "primal")
     gradient = partial_grad.astype(f32).sum(axis=0).astype(bf16)
     gradient = spread(gradient, n_seq, "seq").astype(f32)
@@ -64,21 +143,21 @@
     through = jnp.dot(
         strategy.astype(bf16), seq_payoff, preferred_element_type=f32
     ).astype(bf16)
-    own_strategy = lax.dynamic_slice_in_dim(strategy, seq * width, width, 1)
+    own_strategy = lax.dynamic_slice(
+        strategy, (jnp.uint32(0), own_at), (rows, width)
+    )
 
     player_block = spread(through, n_y, "primal").reshape(-1, width)
-    opp = lax.dot_general(
-        payoff, player_block, (((0,), (0,)), ((), ())), preferred_element_type=f32
-    ).astype(bf16)
-    opp = opp.reshape(n_x * n_zh, 2, rows, width).swapaxes(0, 1)
-    opp = pick(opp, core).astype(f32) + lax.ppermute(
-        pick(opp, 1 - core), "core", SWAP
+    opp = opponent_product(payoff, player_block, n_x * n_zh, rows)
+    opp = pick(opp, core_first).astype(f32) + lax.ppermute(
+        pick(opp, core_second), "core", SWAP
     ).astype(f32)
-    opp = exchange(opp.astype(bf16).reshape(n_x, n_zh * rows, width), "x")
-    opp = opp.astype(f32).sum(axis=0).reshape(n_zh, rows, width)
-    opp_grad = pick(opp, zh) + lax.ppermute(
-        pick(opp, 1 - zh).astype(bf16), "zh", SWAP
+    opp = exchange(opp.astype(bf16).reshape(n_x, n_zh * width, rows), "x")
+    opp = opp.astype(f32).sum(axis=0).reshape(n_zh, width, rows)
+    opp_grad = pick(opp, zh_first) + lax.ppermute(
+        pick(opp, zh_second).astype(bf16), "zh", SWAP
     ).astype(f32)
+    opp_grad = opp_grad.T
     return own_strategy, opp_grad
 
 

time: 148 us -> 136 us (0.919)
  blocking collectives: 71.6 us -> 100 us
  waiting for transfers between devices: 31.7 us -> 8.49 us
  local copies, waits for them, and re-layouts: 9.81 us -> 2.53 us
  starting transfers between devices: 21.7 us -> 15.2 us
  matrix products: 7.13 us -> 2.39 us
  Pallas kernels: 0 us -> 4.51 us
  other arithmetic: 4.23 us -> 1.92 us
    all_to_all x4 -> x6, blocking collectives: 71.6 us -> 100 us  [exchange(): return lax.all_to_all(blocks, axis, split_axis=0, concat_axis=0, tiled=True)]
    all_to_all x2 -> x0, waiting for transfers between devices: 23.9 us -> none  [exchange(): return lax.all_to_all(blocks, axis, split_axis=0, concat_axis=0, tiled=True)]
    all_to_all x2 -> x0, starting transfers between devices: 6.96 us -> none  [exchange(): return lax.all_to_all(blocks, axis, split_axis=0, concat_axis=0, tiled=True)]
    dot_general x2 -> x0, matrix products: 4.75 us -> none  [the longest x1 3.45 us: body(): lax.dot_general(payoff, player_block, (((0,), (0,)), ((), ())), preferred...]
    pallas_call x0 -> x2, Pallas kernels: none -> 4.51 us  [the longest x1 2.75 us: opponent_product(): pl.pallas_call(opponent_kernel, in_specs=[VMEM_SPEC] * 2, out_specs=VMEM_...]
    another operation x1 -> x0, local copies, waits for them, and re-layouts: 3.14 us -> none
    unnamed x8 -> x9, local copies, waits for them, and re-layouts: 4.06 us -> 1.59 us
    convert_element_type x1 -> x2, other arithmetic: 1.96 us -> 0.23 us  [the longest x1 0.21 us: body(): opp = exchange(opp.astype(bf16).reshape(n_x, n_zh * width, rows), 'x')]
  transfers between devices with their start and end apart: 5 -> 3, of which waited for: 5 -> 3; matrix products, arithmetic and copies ran while one was open for 1% -> 1% of each run, Pallas kernels for 0% -> 0%
where the time goes in v4:
time: 136 us
  blocking collectives  100 us (74%)
  starting transfers between devices  15.2 us (11%)
  waiting for transfers between devices  8.49 us (6%)
  Pallas kernels  4.51 us (3%)
  local copies, waits for them, and re-layouts  2.53 us (2%)
  matrix products  2.39 us (2%)
  other arithmetic  1.92 us (1%)
    all_to_all x6, blocking collectives, exchange(): return lax.all_to_all(blocks, axis, split_axis=0, concat_axis=0, tiled=True)  100 us
    ppermute x1, starting transfers between devices, body(): lax.ppermute(pick(opp, core_second), 'core', SWAP).astype(f32)  5.94 us
    ppermute x1, starting transfers between devices, body(): other = lax.ppermute(mixed, 'core', SWAP)  5.78 us
    ppermute x1, waiting for transfers between devices, body(): lax.ppermute(pick(opp, zh_second).astype(bf16), 'zh', SWAP).astype(f32)  5.49 us
    ppermute x1, starting transfers between devices, body(): lax.ppermute(pick(opp, zh_second).astype(bf16), 'zh', SWAP).astype(f32)  3.46 us
    pallas_call x1, Pallas kernels, opponent_product(): pl.pallas_call(opponent_kernel, in_specs=[VMEM_SPEC] * 2, out_specs=VMEM_...  2.75 us
  transfers between devices with their start and end apart: 3, of which 3 were waited for; matrix products, arithmetic and copies ran while one was open for 1% of the time, Pallas kernels for 0%

profile of v4, /device:TPU:1, one launch (start us, length us, event | category | flops | bytes accessed | tf_op | source)
XLA Modules:
  0.0 135.9 jit_solution(4849995255451747042)
XLA Ops:
  0.6 0.0 copy-start
  0.6 0.7 convert_element_type.59
  1.4 0.3 copy-done
  1.7 1.2 fusion.4
  3.0 26.7 %all_to_all.30 = bf16[8,128,256]{2,1,0:T(8,128)(2,1)S(1)} all-to-all(bf16[8,128,256]{2,1,0:T(8,128)(2,1)S(1)} %bitcast.43), channel_id=1, replica_groups=mesh['x'=4,'zh'=2,'core'=2,'primal'=8,'seq'=4] {'zh','seq'}, dimensions={0} | all-to-all | bytes 1048576 | tf_op jit(solution)/shard_map/all_to_all | solution.py:19
  29.6 0.1 bitcast_reduce_fusion
  29.7 10.7 %all_to_all.31 = bf16[4,2,128,256]{3,2,1,0:T(8,128)(2,1)S(1)} all-to-all(bf16[4,2,128,256]{3,2,1,0:T(8,128)(2,1)S(1)} %broadcast_in_dim.9), channel_id=1, replica_groups=mesh['x'=4,'zh'=2,'core'=2,'primal'=8,'seq'=4] {'x'}, dimensions={0} | all-to-all | bytes 1048576 | tf_op jit(solution)/shard_map/all_to_all | solution.py:19
  40.5 5.8 %collective-permute-start = (bf16[8,128,256]{2,1,0:T(8,128)(2,1)S(1)}, bf16[8,128,256]{2,1,0:T(8,128)(2,1)S(1)}, u32[]{:S(2)}, u32[]{:S(2)}) collective-permute-start(bf16[8,128,256]{2,1,0:T(8,128)(2,1)S(1)} %bitcast.41), channel_id=1, source_target_pairs={{0,32},{32,0},{1,33},{33,1},{2,34},{34,2},{3,35},{35,3},{4,36},{36... | collective-permute-start | bytes 1572872 | tf_op jit(solution)/shard_map/ppermute | solution.py:117
  46.3 0.0 copy-start.1
  46.3 1.5 %collective-permute-done = bf16[8,128,256]{2,1,0:T(8,128)(2,1)S(1)} collective-permute-done((bf16[8,128,256]{2,1,0:T(8,128)(2,1)S(1)}, bf16[8,128,256]{2,1,0:T(8,128)(2,1)S(1)}, u32[]{:S(2)}, u32[]{:S(2)}) %collective-permute-start) | collective-permute-done | bytes 524320 | tf_op jit(solution)/shard_map/ppermute | solution.py:117
  47.8 0.1 select_bitcast_fusion.2
  47.9 0.1 pad_maximum_fusion
  48.0 0.5 copy-done.1
  48.5 1.8 %shard_map.68 = bf16[1024,256]{1,0:T(8,128)(2,1)S(1)} custom-call(bf16[1024,2048]{1,0:T(8,128)(2,1)S(1)} %copy-done.1, bf16[2048,256]{1,0:T(8,128)(2,1)S(1)} %bitcast.36), custom_call_target="tpu_custom_call" | custom-call | flops 1073741824 | bytes 4194304 | tf_op jit(solution)/shard_map/pallas_call | solution.py:51
  50.2 0.0 copy-start.3
  50.2 24.6 %all_to_all.32 = bf16[8,128,256]{2,1,0:T(8,128)(2,1)S(1)} all-to-all(bf16[8,128,256]{2,1,0:T(8,128)(2,1)S(1)} %bitcast.37), channel_id=1, replica_groups=mesh['x'=4,'zh'=2,'core'=2,'primal'=8,'seq'=4] {'primal'}, dimensions={0} | all-to-all | bytes 1048576 | tf_op jit(solution)/shard_map/all_to_all | solution.py:19
  74.9 0.1 reduce_sum.34
  75.0 9.6 %all_to_all.33 = bf16[4,128,256]{2,1,0:T(8,128)(2,1)S(1)} all-to-all(bf16[4,128,256]{2,1,0:T(8,128)(2,1)S(1)} %broadcast_in_dim.10), channel_id=1, replica_groups=mesh['x'=4,'zh'=2,'core'=2,'primal'=8,'seq'=4] {'seq'}, dimensions={0} | all-to-all | bytes 524288 | tf_op jit(solution)/shard_map/all_to_all | solution.py:19
  84.5 0.1 fusion.9
  84.7 0.2 fusion.8
  84.9 0.1 subtract_convert_fusion
  85.0 0.0 copy-done.3
  85.0 0.0 copy-start.2
  85.0 0.9 fusion
  86.0 0.1 fusion.10
  86.1 0.2 convolution_convert_fusion.1
  86.4 16.8 %all_to_all.34 = bf16[8,128,256]{2,1,0:T(8,128)(2,1)S(1)} all-to-all(bf16[8,128,256]{2,1,0:T(8,128)(2,1)S(1)} %broadcast_in_dim.11), channel_id=1, replica_groups=mesh['x'=4,'zh'=2,'core'=2,'primal'=8,'seq'=4] {'primal'}, dimensions={0} | all-to-all | bytes 1048576 | tf_op jit(solution)/shard_map/all_to_all | solution.py:19
  103.2 0.0 copy-done.2
  103.2 2.7 %shard_map.69 = bf16[2,8,256,128]{3,2,1,0:T(8,128)(2,1)S(1)} custom-call(bf16[1024,2048]{1,0:T(8,128)(2,1)S(1)} %copy-done.2, bf16[1024,256]{1,0:T(8,128)(2,1)S(1)} %bitcast.38), custom_call_target="tpu_custom_call" | custom-call | flops 1073741824 | bytes 4194304 | tf_op jit(solution)/shard_map/pallas_call | solution.py:82
  105.9 0.1 select_bitcast_fusion
  106.0 5.9 %collective-permute-start.1 = (bf16[8,256,128]{2,1,0:T(8,128)(2,1)S(1)}, bf16[8,256,128]{2,1,0:T(8,128)(2,1)S(1)}, u32[]{:S(2)}, u32[]{:S(2)}) collective-permute-start(bf16[8,256,128]{2,1,0:T(8,128)(2,1)S(1)} %select_bitcast_fusion), channel_id=1, source_target_pairs={{0,32},{32,0},{1,33},{33,1},{2,34},{34,2},{3,35},{35,3},{4,36},{36... | collective-permute-start | bytes 1572872 | tf_op jit(solution)/shard_map/ppermute | solution.py:152
  112.0 1.5 %collective-permute-done.1 = bf16[8,256,128]{2,1,0:T(8,128)(2,1)S(1)} collective-permute-done((bf16[8,256,128]{2,1,0:T(8,128)(2,1)S(1)}, bf16[8,256,128]{2,1,0:T(8,128)(2,1)S(1)}, u32[]{:S(2)}, u32[]{:S(2)}) %collective-permute-start.1) | collective-permute-done | bytes 524320 | tf_op jit(solution)/shard_map/ppermute | solution.py:152
  113.5 0.2 fusion.5
  113.7 11.6 %all_to_all.35 = bf16[4,512,128]{2,1,0:T(8,128)(2,1)S(1)} all-to-all(bf16[4,512,128]{2,1,0:T(8,128)(2,1)S(1)} %bitcast.42), channel_id=1, replica_groups=mesh['x'=4,'zh'=2,'core'=2,'primal'=8,'seq'=4] {'x'}, dimensions={0} | all-to-all | bytes 1048576 | tf_op jit(solution)/shard_map/all_to_all | solution.py:19
  125.3 0.1 convert_reduce_fusion
  125.4 3.5 %collective-permute-start.2 = (bf16[256,128]{1,0:T(8,128)(2,1)S(1)}, bf16[256,128]{1,0:T(8,128)(2,1)S(1)}, u32[]{:S(2)}, u32[]{:S(2)}) collective-permute-start(bf16[256,128]{1,0:T(8,128)(2,1)S(1)} %select_convert_fusion), channel_id=1, source_target_pairs={{0,64},{64,0},{1,65},{65,1},{2,66},{66,2},{3,67},{67,3},{4,68},{68... | collective-permute-start | bytes 196616 | tf_op jit(solution)/shard_map/ppermute | solution.py:157
  128.9 0.8 constant_dynamic-slice_fusion
  129.6 5.5 %collective-permute-done.2 = bf16[256,128]{1,0:T(8,128)(2,1)S(1)} collective-permute-done((bf16[256,128]{1,0:T(8,128)(2,1)S(1)}, bf16[256,128]{1,0:T(8,128)(2,1)S(1)}, u32[]{:S(2)}, u32[]{:S(2)}) %collective-permute-start.2) | collective-permute-done | bytes 65568 | tf_op jit(solution)/shard_map/ppermute | solution.py:157
  135.2 0.8 copy.13
  (8 shorter events, 0.2 us)
Async XLA Ops:
  0.6 1.1 copy-start
  40.5 7.3 %collective-permute-start = (bf16[8,128,256]{2,1,0:T(8,128)(2,1)S(1)}, bf16[8,128,256]{2,1,0:T(8,128)(2,1)S(1)}, u32[]{:S(2)}, u32[]{:S(2)}) collective-permute-start(bf16[8,128,256]{2,1,0:T(8,128)(2,1)S(1)} %bitcast.41), channel_id=1, source_target_pairs={{0,32},{32,0},{1,33},{33,1},{2,34},{34,2},{3,35},{35,3},{4,36},{36... | collective-permute-start | bytes 1572872 | tf_op jit(solution)/shard_map/ppermute | solution.py:117
  46.3 2.2 %copy-start.1 = (bf16[1024,2048]{1,0:T(8,128)(2,1)S(1)}, bf16[1024,2048]{1,0:T(8,128)(2,1)}, u32[]{:S(2)}) copy-start(bf16[1024,2048]{1,0:T(8,128)(2,1)} %payoff_ref.3) | copy-start | bytes 12582916
  50.2 34.8 %copy-start.3 = (s32[1024]{0:T(1024)S(1)}, s32[1024]{0:T(1024)}, u32[]{:S(2)}) copy-start(s32[1024]{0:T(1024)} %param.9) | copy-start | bytes 12292
  85.0 18.2 %copy-start.2 = (bf16[1024,2048]{1,0:T(8,128)(2,1)S(1)}, bf16[1024,2048]{1,0:T(8,128)(2,1)}, u32[]{:S(2)}) copy-start(bf16[1024,2048]{1,0:T(8,128)(2,1)} %payoff_ref.3) | copy-start | bytes 12582916
  106.0 7.5 %collective-permute-start.1 = (bf16[8,256,128]{2,1,0:T(8,128)(2,1)S(1)}, bf16[8,256,128]{2,1,0:T(8,128)(2,1)S(1)}, u32[]{:S(2)}, u32[]{:S(2)}) collective-permute-start(bf16[8,256,128]{2,1,0:T(8,128)(2,1)S(1)} %select_bitcast_fusion), channel_id=1, source_target_pairs={{0,32},{32,0},{1,33},{33,1},{2,34},{34,2},{3,35},{35,3},{4,36},{36... | collective-permute-start | bytes 1572872 | tf_op jit(solution)/shard_map/ppermute | solution.py:152
  125.4 9.7 %collective-permute-start.2 = (bf16[256,128]{1,0:T(8,128)(2,1)S(1)}, bf16[256,128]{1,0:T(8,128)(2,1)S(1)}, u32[]{:S(2)}, u32[]{:S(2)}) collective-permute-start(bf16[256,128]{1,0:T(8,128)(2,1)S(1)} %select_convert_fusion), channel_id=1, source_target_pairs={{0,64},{64,0},{1,65},{65,1},{2,66},{66,2},{3,67},{67,3},{4,68},{68... | collective-permute-start | bytes 196616 | tf_op jit(solution)/shard_map/ppermute | solution.py:157

commit v5 on v4

--- a/solution.py
+++ b/solution.py
@@ -12,6 +12,8 @@
 f32 = jnp.float32
 DUAL = ("x", "zh", "core")
 KERNEL_VMEM = 16 << 20
+PLANE = ("primal", "seq")
+LINE = ("zh", "seq")
 SWAP = ((0, 1), (1, 0))
 
 
@@ -97,9 +99,9 @@
 def body(payoff, opp_strategy, opp_combos, seq_payoff, seq_parent):
     rows, width = opp_strategy.shape
     n_x, n_zh, n_y, n_seq = (lax.axis_size(a) for a in ("x", "zh", "primal", "seq"))
-    core, zh, seq = (lax.axis_index(a) for a in ("core", "zh", "seq"))
-    core_first, zh_first = core == 0, zh == 0
-    core_second, zh_second = core == 1, zh == 1
+    core = lax.axis_index("core")
+    core_first, core_second = core == 0, core == 1
+    part_rows = rows // n_seq
     same = (seq_parent[:, None] == seq_parent[None, :]).astype(bf16)
 
     scaled = (opp_combos.astype(f32)[:, None] * opp_strategy).astype(bf16)
@@ -110,7 +112,7 @@
         preferred_element_type=f32,
     ).astype(bf16)
     part = jnp.broadcast_to(part[None], (n_zh, *part.shape)).reshape(-1, rows, width)
-    part = exchange(part, ("zh", "seq")).reshape(n_zh, n_seq, rows, width)
+    part = exchange(part, LINE).reshape(n_zh, n_seq, rows, width)
     mixed = part.astype(f32).sum(axis=1).astype(bf16)
 
     mixed = spread(mixed, n_x, "x").reshape(n_x * n_zh, rows, width)
@@ -121,43 +123,44 @@
         axis=1,
     )
     partial_grad = player_product(payoff, block.reshape(-1, width))
-    own_at = (seq * width).astype(jnp.uint32)
-    partial_grad, own_at, core_first, core_second, zh_first, zh_second = (
-        lax.optimization_barrier(
-            (partial_grad, own_at, core_first, core_second, zh_first, zh_second)
-        )
+    own_y = lax.axis_index("primal").astype(jnp.uint32)
+    partial_grad, own_y, core_first, core_second = lax.optimization_barrier(
+        (partial_grad, own_y, core_first, core_second)
     )
-    partial_grad = exchange(partial_grad.reshape(n_y, rows, width), "primal")
-    gradient = partial_grad.astype(f32).sum(axis=0).astype(bf16)
-    gradient = spread(gradient, n_seq, "seq").astype(f32)
+    partial_grad = exchange(
+        partial_grad.reshape(n_y * n_seq, part_rows, width), PLANE
+    ).reshape(n_y, n_seq, part_rows, width)
+    gradient = partial_grad.astype(f32).sum(axis=0)
 
     largest = jnp.max(jnp.abs(gradient), axis=(0, 2), keepdims=True)
     exponent = jnp.exp(-logit_span * gradient / (largest + epsilon))
-    exponent = jnp.swapaxes(exponent, 0, 1).reshape(rows, n_seq * width)
+    exponent = jnp.swapaxes(exponent, 0, 1).reshape(part_rows, n_seq * width)
     high = exponent.astype(bf16)
     low = (exponent - high.astype(f32)).astype(bf16)
     totals = jnp.dot(
         jnp.concatenate([high, low], axis=0), same, preferred_element_type=f32
     )
-    strategy = exponent / (totals[:rows] + totals[rows:])
-    through = jnp.dot(
-        strategy.astype(bf16), seq_payoff, preferred_element_type=f32
-    ).astype(bf16)
-    own_strategy = lax.dynamic_slice(
-        strategy, (jnp.uint32(0), own_at), (rows, width)
-    )
+    strategy = (exponent / (totals[:part_rows] + totals[part_rows:])).astype(bf16)
+    strategy = jnp.swapaxes(strategy.reshape(part_rows, n_seq, width), 0, 1)
+    strategy = jnp.broadcast_to(strategy[None], (n_y, *strategy.shape))
+    strategy = exchange(strategy.reshape(n_y * n_seq, part_rows, width), PLANE)
+    strategy = strategy.reshape(n_y, rows, width)
+    own_strategy = lax.dynamic_index_in_dim(strategy, own_y, 0, False).astype(f32)
 
-    player_block = spread(through, n_y, "primal").reshape(-1, width)
-    opp = opponent_product(payoff, player_block, n_x * n_zh, rows)
+    opp = opponent_product(payoff, strategy.reshape(-1, width), n_x * n_zh, rows)
     opp = pick(opp, core_first).astype(f32) + lax.ppermute(
         pick(opp, core_second), "core", SWAP
     ).astype(f32)
-    opp = exchange(opp.astype(bf16).reshape(n_x, n_zh * width, rows), "x")
-    opp = opp.astype(f32).sum(axis=0).reshape(n_zh, width, rows)
-    opp_grad = pick(opp, zh_first) + lax.ppermute(
-        pick(opp, zh_second).astype(bf16), "zh", SWAP
-    ).astype(f32)
-    opp_grad = opp_grad.T
+    opp, own_strategy = lax.optimization_barrier((opp.astype(bf16), own_strategy))
+    opp = exchange(opp.reshape(n_x, n_zh * width, rows), "x")
+    opp = opp.astype(f32).sum(axis=0).astype(bf16).reshape(n_zh, 1, width, rows)
+    opp = jnp.broadcast_to(opp, (n_zh, n_seq, width, rows))
+    opp = exchange(opp.reshape(n_zh * n_seq, width, rows), LINE)
+    opp = opp.reshape(n_zh, n_seq * width, rows)
+    opp = (opp[0].astype(f32) + opp[1].astype(f32)).astype(bf16)
+    opp_grad = lax.dot_general(
+        opp, seq_payoff, (((0,), (0,)), ((), ())), preferred_element_type=f32
+    )
     return own_strategy, opp_grad
 
 

time: 136 us -> 142 us (1.044)
  blocking collectives: 100 us -> 114 us
  waiting for transfers between devices: 8.49 us -> 2.34 us
  starting transfers between devices: 15.2 us -> 10 us
    all_to_all x6, blocking collectives: 100 us -> 114 us  [exchange(): return lax.all_to_all(blocks, axis, split_axis=0, concat_axis=0, tiled=True)]
    ppermute x1 -> x0, waiting for transfers between devices: 5.49 us -> none  [body(): lax.ppermute(pick(opp, zh_second).astype(bf16), 'zh', SWAP).astype(f32)]
    ppermute x1 -> x0, starting transfers between devices: 3.46 us -> none  [body(): lax.ppermute(pick(opp, zh_second).astype(bf16), 'zh', SWAP).astype(f32)]
    ppermute x1, starting transfers between devices: 5.94 us -> 4.23 us  [body(): lax.ppermute(pick(opp, core_second), 'core', SWAP).astype(f32)]
    unnamed x9 -> x8, local copies, waits for them, and re-layouts: 1.59 us -> 3 us
  transfers between devices with their start and end apart: 3 -> 2, of which waited for: 3 -> 2; matrix products, arithmetic and copies ran while one was open for 1% -> 0% of each run, Pallas kernels for 0% -> 0%
where the time goes in v5:
time: 142 us; the launch traced here: 141 us
  blocking collectives  114 us (80%)
  starting transfers between devices  10 us (7%)
  Pallas kernels  4.5 us (3%)
  local copies, waits for them, and re-layouts  3.25 us (2%)
  matrix products  3.01 us (2%)
  other arithmetic  2.43 us (2%)
  waiting for transfers between devices  2.34 us (2%)
    all_to_all x6, blocking collectives, exchange(): return lax.all_to_all(blocks, axis, split_axis=0, concat_axis=0, tiled=True)  114 us
    ppermute x1, starting transfers between devices, body(): other = lax.ppermute(mixed, 'core', SWAP)  5.78 us
    ppermute x1, starting transfers between devices, body(): lax.ppermute(pick(opp, core_second), 'core', SWAP).astype(f32)  4.23 us
    unnamed x8, local copies, waits for them, and re-layouts  3 us
  transfers between devices with their start and end apart: 2, of which 2 were waited for; matrix products, arithmetic and copies ran while one was open for 0% of the time, Pallas kernels for 0%

profile of v5, /device:TPU:1, one launch (start us, length us, event | category | flops | bytes accessed | tf_op | source)
XLA Modules:
  0.0 140.6 jit_solution(11408802884013792407)
XLA Ops:
  0.6 0.0 copy-start
  0.6 0.7 convert_element_type.70
  1.4 0.3 copy-done
  1.7 1.2 fusion.4
  3.0 26.7 %all_to_all.30 = bf16[8,128,256]{2,1,0:T(8,128)(2,1)S(1)} all-to-all(bf16[8,128,256]{2,1,0:T(8,128)(2,1)S(1)} %bitcast.54), channel_id=1, replica_groups=mesh['x'=4,'zh'=2,'core'=2,'primal'=8,'seq'=4] {'zh','seq'}, dimensions={0} | all-to-all | bytes 1048576 | tf_op jit(solution)/shard_map/all_to_all | solution.py:21
  29.6 0.1 bitcast_reduce_fusion
  29.7 10.7 %all_to_all.31 = bf16[4,2,128,256]{3,2,1,0:T(8,128)(2,1)S(1)} all-to-all(bf16[4,2,128,256]{3,2,1,0:T(8,128)(2,1)S(1)} %broadcast_in_dim.11), channel_id=1, replica_groups=mesh['x'=4,'zh'=2,'core'=2,'primal'=8,'seq'=4] {'x'}, dimensions={0} | all-to-all | bytes 1048576 | tf_op jit(solution)/shard_map/all_to_all | solution.py:21
  40.5 5.8 %collective-permute-start = (bf16[8,128,256]{2,1,0:T(8,128)(2,1)S(1)}, bf16[8,128,256]{2,1,0:T(8,128)(2,1)S(1)}, u32[]{:S(2)}, u32[]{:S(2)}) collective-permute-start(bf16[8,128,256]{2,1,0:T(8,128)(2,1)S(1)} %bitcast.50), channel_id=1, source_target_pairs={{0,32},{32,0},{1,33},{33,1},{2,34},{34,2},{3,35},{35,3},{4,36},{36... | collective-permute-start | bytes 1572872 | tf_op jit(solution)/shard_map/ppermute | solution.py:119
  46.3 0.0 copy-start.1
  46.3 1.5 %collective-permute-done = bf16[8,128,256]{2,1,0:T(8,128)(2,1)S(1)} collective-permute-done((bf16[8,128,256]{2,1,0:T(8,128)(2,1)S(1)}, bf16[8,128,256]{2,1,0:T(8,128)(2,1)S(1)}, u32[]{:S(2)}, u32[]{:S(2)}) %collective-permute-start) | collective-permute-done | bytes 524320 | tf_op jit(solution)/shard_map/ppermute | solution.py:119
  47.8 0.1 select_bitcast_fusion.2
  47.9 0.1 pad_maximum_fusion
  48.0 0.5 copy-done.1
  48.5 0.0 copy-start.3
  48.5 1.8 %shard_map.68 = bf16[1024,256]{1,0:T(8,128)(2,1)S(1)} custom-call(bf16[1024,2048]{1,0:T(8,128)(2,1)S(1)} %copy-done.1, bf16[2048,256]{1,0:T(8,128)(2,1)S(1)} %bitcast.46), custom_call_target="tpu_custom_call" | custom-call | flops 1073741824 | bytes 4194304 | tf_op jit(solution)/shard_map/pallas_call | solution.py:53
  50.2 24.4 %all_to_all.32 = bf16[32,32,256]{2,1,0:T(8,128)(2,1)S(1)} all-to-all(bf16[32,32,256]{2,1,0:T(8,128)(2,1)S(1)} %bitcast.49), channel_id=1, replica_groups=mesh['x'=4,'zh'=2,'core'=2,'primal'=8,'seq'=4] {'primal','seq'}, dimensions={0} | all-to-all | bytes 1048576 | tf_op jit(solution)/shard_map/all_to_all | solution.py:21
  74.6 0.1 convert_reduce_fusion
  74.7 0.1 abs_reduce_fusion
  74.8 0.1 exponential_bitcast_fusion
  75.0 0.0 copy-done.3
  75.0 0.9 fusion
  76.0 0.1 broadcast_in_dim.12
  76.0 21.6 %all_to_all.33 = bf16[32,32,256]{2,1,0:T(8,128)(2,1)S(1)} all-to-all(bf16[32,32,256]{2,1,0:T(8,128)(2,1)S(1)} %bitcast.55), channel_id=1, replica_groups=mesh['x'=4,'zh'=2,'core'=2,'primal'=8,'seq'=4] {'primal','seq'}, dimensions={0} | all-to-all | bytes 1048576 | tf_op jit(solution)/shard_map/all_to_all | solution.py:21
  97.6 0.0 copy-start.2
  97.6 2.2 %copy-done.2 = bf16[1024,2048]{1,0:T(8,128)(2,1)S(1)} copy-done((bf16[1024,2048]{1,0:T(8,128)(2,1)S(1)}, bf16[1024,2048]{1,0:T(8,128)(2,1)}, u32[]{:S(2)}) %copy-start.2) | copy-done | bytes 4194328
  99.8 2.7 %shard_map.69 = bf16[2,8,256,128]{3,2,1,0:T(8,128)(2,1)S(1)} custom-call(bf16[1024,2048]{1,0:T(8,128)(2,1)S(1)} %copy-done.2, bf16[1024,256]{1,0:T(8,128)(2,1)S(1)} %bitcast.47), custom_call_target="tpu_custom_call" | custom-call | flops 1073741824 | bytes 4194304 | tf_op jit(solution)/shard_map/pallas_call | solution.py:84
  102.6 0.1 select_bitcast_fusion
  102.7 4.2 %collective-permute-start.1 = (bf16[8,256,128]{2,1,0:T(8,128)(2,1)S(1)}, bf16[8,256,128]{2,1,0:T(8,128)(2,1)S(1)}, u32[]{:S(2)}, u32[]{:S(2)}) collective-permute-start(bf16[8,256,128]{2,1,0:T(8,128)(2,1)S(1)} %select_bitcast_fusion), channel_id=1, source_target_pairs={{0,32},{32,0},{1,33},{33,1},{2,34},{34,2},{3,35},{35,3},{4,36},{36... | collective-permute-start | bytes 1572872 | tf_op jit(solution)/shard_map/ppermute | solution.py:151
  106.9 0.7 bitcast_convert_fusion
  107.6 0.8 collective-permute-done.1
  108.4 0.2 fusion.5
  108.6 11.6 %all_to_all.34 = bf16[4,512,128]{2,1,0:T(8,128)(2,1)S(1)} all-to-all(bf16[4,512,128]{2,1,0:T(8,128)(2,1)S(1)} %bitcast.51), channel_id=1, replica_groups=mesh['x'=4,'zh'=2,'core'=2,'primal'=8,'seq'=4] {'x'}, dimensions={0} | all-to-all | bytes 1048576 | tf_op jit(solution)/shard_map/all_to_all | solution.py:21
  120.3 0.1 reduce_sum.35
  120.3 0.1 broadcast_in_dim.14
  120.4 19.2 %all_to_all.35 = bf16[8,256,128]{2,1,0:T(8,128)(2,1)S(1)} all-to-all(bf16[8,256,128]{2,1,0:T(8,128)(2,1)S(1)} %bitcast.53), channel_id=1, replica_groups=mesh['x'=4,'zh'=2,'core'=2,'primal'=8,'seq'=4] {'zh','seq'}, dimensions={0} | all-to-all | bytes 1048576 | tf_op jit(solution)/shard_map/all_to_all | solution.py:21
  139.6 0.1 add_convert_fusion
  139.7 0.9 fusion.15
  (8 shorter events, 0.2 us)
Async XLA Ops:
  0.6 1.1 copy-start
  40.5 7.3 %collective-permute-start = (bf16[8,128,256]{2,1,0:T(8,128)(2,1)S(1)}, bf16[8,128,256]{2,1,0:T(8,128)(2,1)S(1)}, u32[]{:S(2)}, u32[]{:S(2)}) collective-permute-start(bf16[8,128,256]{2,1,0:T(8,128)(2,1)S(1)} %bitcast.50), channel_id=1, source_target_pairs={{0,32},{32,0},{1,33},{33,1},{2,34},{34,2},{3,35},{35,3},{4,36},{36... | collective-permute-start | bytes 1572872 | tf_op jit(solution)/shard_map/ppermute | solution.py:119
  46.3 2.2 %copy-start.1 = (bf16[1024,2048]{1,0:T(8,128)(2,1)S(1)}, bf16[1024,2048]{1,0:T(8,128)(2,1)}, u32[]{:S(2)}) copy-start(bf16[1024,2048]{1,0:T(8,128)(2,1)} %payoff_ref.3) | copy-start | bytes 12582916
  48.5 26.5 %copy-start.3 = (s32[1024]{0:T(1024)S(1)}, s32[1024]{0:T(1024)}, u32[]{:S(2)}) copy-start(s32[1024]{0:T(1024)} %param.9) | copy-start | bytes 12292
  97.6 2.2 %copy-start.2 = (bf16[1024,2048]{1,0:T(8,128)(2,1)S(1)}, bf16[1024,2048]{1,0:T(8,128)(2,1)}, u32[]{:S(2)}) copy-start(bf16[1024,2048]{1,0:T(8,128)(2,1)} %payoff_ref.3) | copy-start | bytes 12582916
  102.7 5.8 %collective-permute-start.1 = (bf16[8,256,128]{2,1,0:T(8,128)(2,1)S(1)}, bf16[8,256,128]{2,1,0:T(8,128)(2,1)S(1)}, u32[]{:S(2)}, u32[]{:S(2)}) collective-permute-start(bf16[8,256,128]{2,1,0:T(8,128)(2,1)S(1)} %select_bitcast_fusion), channel_id=1, source_target_pairs={{0,32},{32,0},{1,33},{33,1},{2,34},{34,2},{3,35},{35,3},{4,36},{36... | collective-permute-start | bytes 1572872 | tf_op jit(solution)/shard_map/ppermute | solution.py:151

commit v6 on v4

--- a/solution.py
+++ b/solution.py
@@ -1,3 +1,5 @@
+import functools
+
 import jax
 import jax.numpy as jnp
 from jax import lax
@@ -11,6 +13,7 @@
 bf16 = jnp.bfloat16
 f32 = jnp.float32
 DUAL = ("x", "zh", "core")
+NI = 256
 KERNEL_VMEM = 16 << 20
 SWAP = ((0, 1), (1, 0))
 
@@ -62,36 +65,100 @@
     )(resident(payoff), block)
 
 
-def opponent_kernel(payoff_ref, block_ref, out_ref, turned):
-    turned[...] = block_ref[...].T
-    chips, width, rows = out_ref.shape[1:]
-
-    @pl.loop(0, chips)
-    def _(chip):
-        at = pl.ds(pl.multiple_of(chip * 2 * rows, 2 * rows), 2 * rows)
+def opponent_kernel(core_ref, payoff_ref, block_ref, out_ref, turned):
+    parts, _, part = block_ref.shape
+    for i in range(parts):
+        turned[:, i * part : (i + 1) * part] = block_ref[i]
+    chips, _, rows = out_ref.shape
+    core = core_ref[0]
+
+    def strip(chip):
+        at = pl.multiple_of((2 * chip + core) * rows, rows)
+        return payoff_ref[:, pl.ds(at, rows)]
+
+    @pl.loop(0, chips // 2)
+    def _(i):
         total = jnp.dot(
-            turned[...], payoff_ref[:, at], preferred_element_type=f32
+            turned[...],
+            jnp.concatenate([strip(2 * i), strip(2 * i + 1)], axis=1),
+            preferred_element_type=f32,
         ).astype(bf16)
-        out_ref[0, chip] = total[:, :rows]
-        out_ref[1, chip] = total[:, rows:]
-
-
-def opponent_product(payoff, block, chips, rows):
+        out_ref[2 * i] = total[:, :rows]
+        out_ref[2 * i + 1] = total[:, rows:]
+
+
+def opponent_product(core, payoff, block, chips, rows):
     depth, n_cols = payoff.shape
     width = block.shape[1]
     return pl.pallas_call(
         opponent_kernel,
-        in_specs=[VMEM_SPEC] * 2,
+        in_specs=[pl.BlockSpec(memory_space=pltpu.SMEM)] + [VMEM_SPEC] * 2,
         out_specs=VMEM_SPEC,
-        out_shape=jax.ShapeDtypeStruct((2, chips, width, rows), bf16),
+        out_shape=jax.ShapeDtypeStruct((chips, width, rows), bf16),
         scratch_shapes=[pltpu.VMEM((width, depth), bf16)],
         compiler_params=pltpu.CompilerParams(vmem_limit_bytes=KERNEL_VMEM),
         cost_estimate=pl.CostEstimate(
-            flops=2 * n_cols * depth * width,
-            bytes_accessed=2 * n_cols * depth,
+            flops=n_cols * depth * width,
+            bytes_accessed=n_cols * depth,
             transcendentals=0,
         ),
-    )(resident(payoff), block)
+    )(core[None], resident(payoff), block)
+
+
+def prox_kernel(
+    seq_ref, gradient_ref, seq_payoff_ref, parent_ref, through_ref, own_ref, all_ref
+):
+    n_seq, rows, width = gradient_ref.shape
+    gradient = [gradient_ref[i].astype(f32) for i in range(n_seq)]
+    largest = functools.reduce(jnp.maximum, [jnp.abs(g) for g in gradient])
+    largest = jnp.max(largest, axis=1, keepdims=True)
+    exponent = jnp.exp(
+        -logit_span * jnp.concatenate(gradient, axis=1) / (largest + epsilon)
+    )
+
+    def halves(value):
+        high = value.astype(bf16)
+        low = (value - high.astype(f32)).astype(bf16)
+        return jnp.concatenate([high, low], axis=0)
+
+    infosets = lax.broadcasted_iota(jnp.int32, (NI, n_seq * width), 0)
+    member = (infosets == parent_ref[...]).astype(f32).astype(bf16)
+    totals = lax.dot_general(
+        halves(exponent), member, (((1,), (1,)), ((), ())), preferred_element_type=f32
+    )
+    totals = jnp.dot(
+        halves(totals[:rows] + totals[rows:]), member, preferred_element_type=f32
+    )
+    strategy = exponent / (totals[:rows] + totals[rows:])
+    for i in range(n_seq):
+        all_ref[i] = strategy[:, i * width : (i + 1) * width]
+    own_ref[...] = all_ref[seq_ref[0]]
+    through = jnp.dot(
+        strategy.astype(bf16), seq_payoff_ref[...], preferred_element_type=f32
+    )
+    through = through.T.astype(bf16)
+    for i in range(through_ref.shape[0]):
+        through_ref[i] = through
+
+
+def prox(seq, gradient, seq_payoff, seq_parent, copies):
+    n_seq, rows, width = gradient.shape
+    return pl.pallas_call(
+        prox_kernel,
+        in_specs=[pl.BlockSpec(memory_space=pltpu.SMEM)] + [VMEM_SPEC] * 3,
+        out_specs=(VMEM_SPEC, VMEM_SPEC),
+        out_shape=(
+            jax.ShapeDtypeStruct((copies, width, rows), bf16),
+            jax.ShapeDtypeStruct((rows, width), f32),
+        ),
+        scratch_shapes=[pltpu.VMEM((n_seq, rows, width), f32)],
+        compiler_params=pltpu.CompilerParams(vmem_limit_bytes=KERNEL_VMEM),
+        cost_estimate=pl.CostEstimate(
+            flops=64 * n_seq * rows * width * NI,
+            bytes_accessed=2 * seq_payoff.size,
+            transcendentals=n_seq * rows * width,
+        ),
+    )(seq[None], gradient, seq_payoff, seq_parent[None])
 
 
 def body(payoff, opp_strategy, opp_combos, seq_payoff, seq_parent):
@@ -99,8 +166,7 @@
     n_x, n_zh, n_y, n_seq = (lax.axis_size(a) for a in ("x", "zh", "primal", "seq"))
     core, zh, seq = (lax.axis_index(a) for a in ("core", "zh", "seq"))
     core_first, zh_first = core == 0, zh == 0
-    core_second, zh_second = core == 1, zh == 1
-    same = (seq_parent[:, None] == seq_parent[None, :]).astype(bf16)
+    zh_second = zh == 1
 
     scaled = (opp_combos.astype(f32)[:, None] * opp_strategy).astype(bf16)
     part = jnp.einsum(
@@ -121,37 +187,19 @@
         axis=1,
     )
     partial_grad = player_product(payoff, block.reshape(-1, width))
-    own_at = (seq * width).astype(jnp.uint32)
-    partial_grad, own_at, core_first, core_second, zh_first, zh_second = (
-        lax.optimization_barrier(
-            (partial_grad, own_at, core_first, core_second, zh_first, zh_second)
-        )
+    partial_grad, core, mate, seq, zh_first, zh_second = lax.optimization_barrier(
+        (partial_grad, core, 1 - core, seq, zh_first, zh_second)
     )
     partial_grad = exchange(partial_grad.reshape(n_y, rows, width), "primal")
     gradient = partial_grad.astype(f32).sum(axis=0).astype(bf16)
-    gradient = spread(gradient, n_seq, "seq").astype(f32)
-
-    largest = jnp.max(jnp.abs(gradient), axis=(0, 2), keepdims=True)
-    exponent = jnp.exp(-logit_span * gradient / (largest + epsilon))
-    exponent = jnp.swapaxes(exponent, 0, 1).reshape(rows, n_seq * width)
-    high = exponent.astype(bf16)
-    low = (exponent - high.astype(f32)).astype(bf16)
-    totals = jnp.dot(
-        jnp.concatenate([high, low], axis=0), same, preferred_element_type=f32
-    )
-    strategy = exponent / (totals[:rows] + totals[rows:])
-    through = jnp.dot(
-        strategy.astype(bf16), seq_payoff, preferred_element_type=f32
-    ).astype(bf16)
-    own_strategy = lax.dynamic_slice(
-        strategy, (jnp.uint32(0), own_at), (rows, width)
-    )
-
-    player_block = spread(through, n_y, "primal").reshape(-1, width)
-    opp = opponent_product(payoff, player_block, n_x * n_zh, rows)
-    opp = pick(opp, core_first).astype(f32) + lax.ppermute(
-        pick(opp, core_second), "core", SWAP
-    ).astype(f32)
+    gradient = spread(gradient, n_seq, "seq")
+    through, own_strategy = prox(seq, gradient, seq_payoff, seq_parent, n_y)
+
+    through = exchange(through, "primal")
+    away = opponent_product(mate, payoff, through, n_x * n_zh, rows)
+    away = lax.ppermute(away, "core", SWAP)
+    opp = opponent_product(core, payoff, through, n_x * n_zh, rows)
+    opp = opp.astype(f32) + away.astype(f32)
     opp = exchange(opp.astype(bf16).reshape(n_x, n_zh * width, rows), "x")
     opp = opp.astype(f32).sum(axis=0).reshape(n_zh, width, rows)
     opp_grad = pick(opp, zh_first) + lax.ppermute(

time: 136 us -> 135 us (level)
  Pallas kernels: 4.51 us -> 6.59 us
    pallas_call x1 -> x3, Pallas kernels: 2.75 us -> 4.83 us  [the longest x2 3.34 us: opponent_product(): pl.pallas_call(opponent_kernel, in_specs=[pl.BlockSpec(memory_space=pltpu...]
    ppermute x1, waiting for transfers between devices: 1.51 us -> 0.01 us  [body(): away = lax.ppermute(away, 'core', SWAP)]
  transfers between devices with their start and end apart: 3 -> 3, of which waited for: 3 -> 2; matrix products, arithmetic and copies ran while one was open for 1% -> 0% of each run, Pallas kernels for 0% -> 1%
where the time goes in v6:
time: 135 us; the launch traced here: 134 us
  blocking collectives  100 us (74%)
  starting transfers between devices  15.2 us (11%)
  waiting for transfers between devices  7.75 us (6%)
  Pallas kernels  6.59 us (5%)
  matrix products  1.42 us (1%)
    all_to_all x6, blocking collectives, exchange(): return lax.all_to_all(blocks, axis, split_axis=0, concat_axis=0, tiled=True)  100 us
    ppermute x1, waiting for transfers between devices, body(): lax.ppermute(pick(opp, zh_second).astype(bf16), 'zh', SWAP).astype(f32)  6.25 us
    ppermute x1, starting transfers between devices, body(): away = lax.ppermute(away, 'core', SWAP)  5.95 us
    ppermute x1, starting transfers between devices, body(): other = lax.ppermute(mixed, 'core', SWAP)  5.78 us
    ppermute x1, starting transfers between devices, body(): lax.ppermute(pick(opp, zh_second).astype(bf16), 'zh', SWAP).astype(f32)  3.46 us
    pallas_call x2, Pallas kernels, opponent_product(): pl.pallas_call(opponent_kernel, in_specs=[pl.BlockSpec(memory_space=pltpu...  3.34 us
  transfers between devices with their start and end apart: 3, of which 2 were waited for; matrix products, arithmetic and copies ran while one was open for 0% of the time, Pallas kernels for 1%

profile of v6, /device:TPU:1, one launch (start us, length us, event | category | flops | bytes accessed | tf_op | source)
XLA Modules:
  0.0 134.4 jit_solution(7019486358760950714)
XLA Ops:
  0.6 0.7 convert_element_type.34
  1.3 1.4 %fusion = bf16[4,128,256]{2,1,0:T(8,128)(2,1)S(1)} fusion(bf16[4,256,256]{2,1,0:T(8,128)(2,1)} %bitcast.30, f32[128,256]{1,0:T(8,128)} %param.6, f32[128]{0:T(128)S(1)} %convert_element_type.34), kind=kOutput, calls=%fused_computation.1 | convolution fusion | flops 67305472 | bytes 918016 | tf_op jit(solution)/shard_map/bt,zst->zbs/dot_general | solution.py:172
  2.8 26.7 %all_to_all.30 = bf16[8,128,256]{2,1,0:T(8,128)(2,1)S(1)} all-to-all(bf16[8,128,256]{2,1,0:T(8,128)(2,1)S(1)} %bitcast.34), channel_id=1, replica_groups=mesh['x'=4,'zh'=2,'core'=2,'primal'=8,'seq'=4] {'zh','seq'}, dimensions={0} | all-to-all | bytes 1048576 | tf_op jit(solution)/shard_map/all_to_all | solution.py:22
  29.4 0.1 bitcast_reduce_fusion
  29.5 10.7 %all_to_all.31 = bf16[4,2,128,256]{3,2,1,0:T(8,128)(2,1)S(1)} all-to-all(bf16[4,2,128,256]{3,2,1,0:T(8,128)(2,1)S(1)} %broadcast_in_dim.15), channel_id=1, replica_groups=mesh['x'=4,'zh'=2,'core'=2,'primal'=8,'seq'=4] {'x'}, dimensions={0} | all-to-all | bytes 1048576 | tf_op jit(solution)/shard_map/all_to_all | solution.py:22
  40.3 5.8 %collective-permute-start = (bf16[8,128,256]{2,1,0:T(8,128)(2,1)S(1)}, bf16[8,128,256]{2,1,0:T(8,128)(2,1)S(1)}, u32[]{:S(2)}, u32[]{:S(2)}) collective-permute-start(bf16[8,128,256]{2,1,0:T(8,128)(2,1)S(1)} %bitcast.32), channel_id=1, source_target_pairs={{0,32},{32,0},{1,33},{33,1},{2,34},{34,2},{3,35},{35,3},{4,36},{36... | collective-permute-start | bytes 1572872 | tf_op jit(solution)/shard_map/ppermute | solution.py:183
  46.1 0.0 copy-start
  46.1 1.5 %collective-permute-done = bf16[8,128,256]{2,1,0:T(8,128)(2,1)S(1)} collective-permute-done((bf16[8,128,256]{2,1,0:T(8,128)(2,1)S(1)}, bf16[8,128,256]{2,1,0:T(8,128)(2,1)S(1)}, u32[]{:S(2)}, u32[]{:S(2)}) %collective-permute-start) | collective-permute-done | bytes 524320 | tf_op jit(solution)/shard_map/ppermute | solution.py:183
  47.6 0.1 select_bitcast_fusion.1
  47.7 0.1 pad_maximum_fusion
  47.8 0.0 copy-start.2
  47.8 0.0 copy-start.3
  47.8 0.4 copy-done
  48.3 1.8 %shard_map.68 = bf16[1024,256]{1,0:T(8,128)(2,1)S(1)} custom-call(bf16[1024,2048]{1,0:T(8,128)(2,1)S(1)} %copy-done, bf16[2048,256]{1,0:T(8,128)(2,1)S(1)} %bitcast.28), custom_call_target="tpu_custom_call" | custom-call | flops 1073741824 | bytes 4194304 | tf_op jit(solution)/shard_map/pallas_call | solution.py:54
  50.0 24.6 %all_to_all.32 = bf16[8,128,256]{2,1,0:T(8,128)(2,1)S(1)} all-to-all(bf16[8,128,256]{2,1,0:T(8,128)(2,1)S(1)} %bitcast.29), channel_id=1, replica_groups=mesh['x'=4,'zh'=2,'core'=2,'primal'=8,'seq'=4] {'primal'}, dimensions={0} | all-to-all | bytes 1048576 | tf_op jit(solution)/shard_map/all_to_all | solution.py:22
  74.6 0.1 reduce_sum.34
  74.7 9.6 %all_to_all.33.gradient_ref = bf16[4,128,256]{2,1,0:T(8,128)(2,1)S(1)} all-to-all(bf16[4,128,256]{2,1,0:T(8,128)(2,1)S(1)} %broadcast_in_dim.34), channel_id=1, replica_groups=mesh['x'=4,'zh'=2,'core'=2,'primal'=8,'seq'=4] {'seq'}, dimensions={0} | all-to-all | bytes 524288 | tf_op jit(solution)/shard_map/all_to_all | solution.py:22
  84.3 0.0 copy-done.2
  84.3 0.0 copy-done.3
  84.3 0.0 copy-start.1
  84.3 1.5 %shard_map.69 = (bf16[8,256,128]{2,1,0:T(8,128)(2,1)S(1)}, f32[128,256]{1,0:T(8,128)}) custom-call(s32[1]{0:T(128)} %bitcast.10.seq_ref, bf16[4,128,256]{2,1,0:T(8,128)(2,1)S(1)} %all_to_all.33.gradient_ref, bf16[1024,256]{1,0:T(8,128)(2,1)S(1)} %copy-done.2, s32[1,1024]{1,0:T(1,128)S(1)} %bitcast.31), custom_call_target="tpu_custom_call" | custom-call | flops 2147483648 | bytes 524288 | tf_op jit(solution)/shard_map/pallas_call | solution.py:146
  85.8 16.8 %all_to_all.34.block_ref = bf16[8,256,128]{2,1,0:T(8,128)(2,1)S(1)} all-to-all(bf16[8,256,128]{2,1,0:T(8,128)(2,1)S(1)} %get-tuple-element.15), channel_id=1, replica_groups=mesh['x'=4,'zh'=2,'core'=2,'primal'=8,'seq'=4] {'primal'}, dimensions={0} | all-to-all | bytes 1048576 | tf_op jit(solution)/shard_map/all_to_all | solution.py:22
  102.6 0.0 copy-done.1
  102.7 1.7 %shard_map.71 = bf16[8,256,128]{2,1,0:T(8,128)(2,1)S(1)} custom-call(s32[1]{0:T(128)} %bitcast.14.core_ref, bf16[1024,2048]{1,0:T(8,128)(2,1)S(1)} %copy-done.1, bf16[8,256,128]{2,1,0:T(8,128)(2,1)S(1)} %all_to_all.34.block_ref), custom_call_target="tpu_custom_call" | custom-call | flops 536870912 | bytes 2097152 | tf_op jit(solution)/shard_map/pallas_call | solution.py:93
  104.3 5.9 %collective-permute-start.1 = (bf16[8,256,128]{2,1,0:T(8,128)(2,1)S(1)}, bf16[8,256,128]{2,1,0:T(8,128)(2,1)S(1)}, u32[]{:S(2)}, u32[]{:S(2)}) collective-permute-start(bf16[8,256,128]{2,1,0:T(8,128)(2,1)S(1)} %shard_map.71), channel_id=1, source_target_pairs={{0,32},{32,0},{1,33},{33,1},{2,34},{34,2},{3,35},{35,3},{4,36},{36... | collective-permute-start | bytes 1572872 | tf_op jit(solution)/shard_map/ppermute | solution.py:200
  110.3 1.7 %shard_map.70 = bf16[8,256,128]{2,1,0:T(8,128)(2,1)S(1)} custom-call(s32[1]{0:T(128)} %bitcast.13.core_ref, bf16[1024,2048]{1,0:T(8,128)(2,1)S(1)} %copy-done.1, bf16[8,256,128]{2,1,0:T(8,128)(2,1)S(1)} %all_to_all.34.block_ref), custom_call_target="tpu_custom_call" | custom-call | flops 536870912 | bytes 2097152 | tf_op jit(solution)/shard_map/pallas_call | solution.py:93
  112.0 0.0 collective-permute-done.1
  112.0 0.1 add_convert_fusion
  112.1 11.6 %all_to_all.35 = bf16[4,512,128]{2,1,0:T(8,128)(2,1)S(1)} all-to-all(bf16[4,512,128]{2,1,0:T(8,128)(2,1)S(1)} %bitcast.33), channel_id=1, replica_groups=mesh['x'=4,'zh'=2,'core'=2,'primal'=8,'seq'=4] {'x'}, dimensions={0} | all-to-all | bytes 1048576 | tf_op jit(solution)/shard_map/all_to_all | solution.py:22
  123.8 0.1 convert_reduce_fusion
  123.9 3.5 %collective-permute-start.2 = (bf16[256,128]{1,0:T(8,128)(2,1)S(1)}, bf16[256,128]{1,0:T(8,128)(2,1)S(1)}, u32[]{:S(2)}, u32[]{:S(2)}) collective-permute-start(bf16[256,128]{1,0:T(8,128)(2,1)S(1)} %select_convert_fusion), channel_id=1, source_target_pairs={{0,64},{64,0},{1,65},{65,1},{2,66},{66,2},{3,67},{67,3},{4,68},{68... | collective-permute-start | bytes 196616 | tf_op jit(solution)/shard_map/ppermute | solution.py:205
  127.3 6.3 %collective-permute-done.2 = bf16[256,128]{1,0:T(8,128)(2,1)S(1)} collective-permute-done((bf16[256,128]{1,0:T(8,128)(2,1)S(1)}, bf16[256,128]{1,0:T(8,128)(2,1)S(1)}, u32[]{:S(2)}, u32[]{:S(2)}) %collective-permute-start.2) | collective-permute-done | bytes 65568 | tf_op jit(solution)/shard_map/ppermute | solution.py:205
  133.6 0.8 copy.11
  (5 shorter events, 0.1 us)
Async XLA Ops:
  40.3 7.3 %collective-permute-start = (bf16[8,128,256]{2,1,0:T(8,128)(2,1)S(1)}, bf16[8,128,256]{2,1,0:T(8,128)(2,1)S(1)}, u32[]{:S(2)}, u32[]{:S(2)}) collective-permute-start(bf16[8,128,256]{2,1,0:T(8,128)(2,1)S(1)} %bitcast.32), channel_id=1, source_target_pairs={{0,32},{32,0},{1,33},{33,1},{2,34},{34,2},{3,35},{35,3},{4,36},{36... | collective-permute-start | bytes 1572872 | tf_op jit(solution)/shard_map/ppermute | solution.py:183
  46.1 2.2 %copy-start = (bf16[1024,2048]{1,0:T(8,128)(2,1)S(1)}, bf16[1024,2048]{1,0:T(8,128)(2,1)}, u32[]{:S(2)}) copy-start(bf16[1024,2048]{1,0:T(8,128)(2,1)} %payoff_ref.5) | copy-start | bytes 12582916
  47.8 36.5 %copy-start.2 = (bf16[1024,256]{1,0:T(8,128)(2,1)S(1)}, bf16[1024,256]{1,0:T(8,128)(2,1)}, u32[]{:S(2)}) copy-start(bf16[1024,256]{1,0:T(8,128)(2,1)} %seq_payoff_ref.1) | copy-start | bytes 1572868
  47.8 36.5 %copy-start.3 = (s32[1024]{0:T(1024)S(1)}, s32[1024]{0:T(1024)}, u32[]{:S(2)}) copy-start(s32[1024]{0:T(1024)} %param.9) | copy-start | bytes 12292
  84.3 18.3 %copy-start.1 = (bf16[1024,2048]{1,0:T(8,128)(2,1)S(1)}, bf16[1024,2048]{1,0:T(8,128)(2,1)}, u32[]{:S(2)}) copy-start(bf16[1024,2048]{1,0:T(8,128)(2,1)} %payoff_ref.5) | copy-start | bytes 12582916
  104.3 7.6 %collective-permute-start.1 = (bf16[8,256,128]{2,1,0:T(8,128)(2,1)S(1)}, bf16[8,256,128]{2,1,0:T(8,128)(2,1)S(1)}, u32[]{:S(2)}, u32[]{:S(2)}) collective-permute-start(bf16[8,256,128]{2,1,0:T(8,128)(2,1)S(1)} %shard_map.71), channel_id=1, source_target_pairs={{0,32},{32,0},{1,33},{33,1},{2,34},{34,2},{3,35},{35,3},{4,36},{36... | collective-permute-start | bytes 1572872 | tf_op jit(solution)/shard_map/ppermute | solution.py:200
  123.9 9.7 %collective-permute-start.2 = (bf16[256,128]{1,0:T(8,128)(2,1)S(1)}, bf16[256,128]{1,0:T(8,128)(2,1)S(1)}, u32[]{:S(2)}, u32[]{:S(2)}) collective-permute-start(bf16[256,128]{1,0:T(8,128)(2,1)S(1)} %select_convert_fusion), channel_id=1, source_target_pairs={{0,64},{64,0},{1,65},{65,1},{2,66},{66,2},{3,67},{67,3},{4,68},{68... | collective-permute-start | bytes 196616 | tf_op jit(solution)/shard_map/ppermute | solution.py:205

commit v7 on v6

--- a/solution.py
+++ b/solution.py
@@ -69,22 +69,22 @@
     parts, _, part = block_ref.shape
     for i in range(parts):
         turned[:, i * part : (i + 1) * part] = block_ref[i]
-    chips, _, rows = out_ref.shape
+    _, chips, _, rows = out_ref.shape
     core = core_ref[0]
 
     def strip(chip):
         at = pl.multiple_of((2 * chip + core) * rows, rows)
         return payoff_ref[:, pl.ds(at, rows)]
 
-    @pl.loop(0, chips // 2)
+    @pl.loop(0, chips)
     def _(i):
         total = jnp.dot(
             turned[...],
             jnp.concatenate([strip(2 * i), strip(2 * i + 1)], axis=1),
             preferred_element_type=f32,
         ).astype(bf16)
-        out_ref[2 * i] = total[:, :rows]
-        out_ref[2 * i + 1] = total[:, rows:]
+        out_ref[0, i] = total[:, :rows]
+        out_ref[1, i] = total[:, rows:]
 
 
 def opponent_product(core, payoff, block, chips, rows):
@@ -94,7 +94,7 @@
         opponent_kernel,
         in_specs=[pl.BlockSpec(memory_space=pltpu.SMEM)] + [VMEM_SPEC] * 2,
         out_specs=VMEM_SPEC,
-        out_shape=jax.ShapeDtypeStruct((chips, width, rows), bf16),
+        out_shape=jax.ShapeDtypeStruct((2, chips // 2, width, rows), bf16),
         scratch_shapes=[pltpu.VMEM((width, depth), bf16)],
         compiler_params=pltpu.CompilerParams(vmem_limit_bytes=KERNEL_VMEM),
         cost_estimate=pl.CostEstimate(
@@ -199,14 +199,12 @@
     away = opponent_product(mate, payoff, through, n_x * n_zh, rows)
     away = lax.ppermute(away, "core", SWAP)
     opp = opponent_product(core, payoff, through, n_x * n_zh, rows)
-    opp = opp.astype(f32) + away.astype(f32)
-    opp = exchange(opp.astype(bf16).reshape(n_x, n_zh * width, rows), "x")
-    opp = opp.astype(f32).sum(axis=0).reshape(n_zh, width, rows)
-    opp_grad = pick(opp, zh_first) + lax.ppermute(
-        pick(opp, zh_second).astype(bf16), "zh", SWAP
-    ).astype(f32)
-    opp_grad = opp_grad.T
-    return own_strategy, opp_grad
+    opp = (opp.astype(f32) + away.astype(f32)).astype(bf16)
+    far = exchange(pick(opp, zh_second), "x")
+    far, near = lax.optimization_barrier((far, pick(opp, zh_first)))
+    far = lax.ppermute(far.astype(f32).sum(axis=0).astype(bf16), "zh", SWAP)
+    near = exchange(near, "x").astype(f32).sum(axis=0)
+    return own_strategy, (near + far.astype(f32)).T
 
 
 def solution(mesh):

time: 135 us -> 137 us (1.015)
  starting transfers between devices: 15.2 us -> 18.6 us
  blocking collectives: 100 us -> 97.2 us
    all_to_all x0 -> x1, starting transfers between devices: none -> 3.4 us  [exchange(): return lax.all_to_all(blocks, axis, split_axis=0, concat_axis=0, tiled=True)]
    all_to_all x6, blocking collectives: 100 us -> 97.2 us  [exchange(): return lax.all_to_all(blocks, axis, split_axis=0, concat_axis=0, tiled=True)]
    ppermute x1, waiting for transfers between devices: 6.25 us -> 4.24 us  [body(): far = lax.ppermute(far.astype(f32).sum(axis=0).astype(bf16), 'zh', SWAP)]
    all_to_all x0 -> x1, waiting for transfers between devices: none -> 1.98 us  [exchange(): return lax.all_to_all(blocks, axis, split_axis=0, concat_axis=0, tiled=True)]
  transfers between devices with their start and end apart: 3 -> 4, of which waited for: 2 -> 3; matrix products, arithmetic and copies ran while one was open for 0% -> 0% of each run, Pallas kernels for 1% -> 1%
where the time goes in v7:
time: 137 us; the launch traced here: 136 us
  blocking collectives  97.2 us (71%)
  starting transfers between devices  18.6 us (14%)
  waiting for transfers between devices  7.71 us (6%)
  Pallas kernels  6.59 us (5%)
  other arithmetic  1.98 us (1%)
  matrix products  1.42 us (1%)
    all_to_all x6, blocking collectives, exchange(): return lax.all_to_all(blocks, axis, split_axis=0, concat_axis=0, tiled=True)  97.2 us
    ppermute x1, starting transfers between devices, body(): away = lax.ppermute(away, 'core', SWAP)  5.95 us
    ppermute x1, starting transfers between devices, body(): other = lax.ppermute(mixed, 'core', SWAP)  5.78 us
    ppermute x1, waiting for transfers between devices, body(): far = lax.ppermute(far.astype(f32).sum(axis=0).astype(bf16), 'zh', SWAP)  4.24 us
    ppermute x1, starting transfers between devices, body(): far = lax.ppermute(far.astype(f32).sum(axis=0).astype(bf16), 'zh', SWAP)  3.46 us
    all_to_all x1, starting transfers between devices, exchange(): return lax.all_to_all(blocks, axis, split_axis=0, concat_axis=0, tiled=True)  3.4 us
    pallas_call x2, Pallas kernels, opponent_product(): pl.pallas_call(opponent_kernel, in_specs=[pl.BlockSpec(memory_space=pltpu...  3.34 us
  transfers between devices with their start and end apart: 4, of which 3 were waited for; matrix products, arithmetic and copies ran while one was open for 0% of the time, Pallas kernels for 1%

profile of v7, /device:TPU:1, one launch (start us, length us, event | category | flops | bytes accessed | tf_op | source)
XLA Modules:
  0.0 135.6 jit_solution(15618860780318746914)
XLA Ops:
  0.6 0.7 convert_element_type.33
  1.3 1.4 %fusion = bf16[4,128,256]{2,1,0:T(8,128)(2,1)S(1)} fusion(bf16[4,256,256]{2,1,0:T(8,128)(2,1)} %bitcast.33, f32[128,256]{1,0:T(8,128)} %param.6, f32[128]{0:T(128)S(1)} %convert_element_type.33), kind=kOutput, calls=%fused_computation.1 | convolution fusion | flops 67305472 | bytes 918016 | tf_op jit(solution)/shard_map/bt,zst->zbs/dot_general | solution.py:172
  2.8 26.7 %all_to_all.35 = bf16[8,128,256]{2,1,0:T(8,128)(2,1)S(1)} all-to-all(bf16[8,128,256]{2,1,0:T(8,128)(2,1)S(1)} %bitcast.36), channel_id=1, replica_groups=mesh['x'=4,'zh'=2,'core'=2,'primal'=8,'seq'=4] {'zh','seq'}, dimensions={0} | all-to-all | bytes 1048576 | tf_op jit(solution)/shard_map/all_to_all | solution.py:22
  29.4 0.1 bitcast_reduce_fusion
  29.5 10.7 %all_to_all.36 = bf16[4,2,128,256]{3,2,1,0:T(8,128)(2,1)S(1)} all-to-all(bf16[4,2,128,256]{3,2,1,0:T(8,128)(2,1)S(1)} %broadcast_in_dim.15), channel_id=1, replica_groups=mesh['x'=4,'zh'=2,'core'=2,'primal'=8,'seq'=4] {'x'}, dimensions={0} | all-to-all | bytes 1048576 | tf_op jit(solution)/shard_map/all_to_all | solution.py:22
  40.3 5.8 %collective-permute-start = (bf16[8,128,256]{2,1,0:T(8,128)(2,1)S(1)}, bf16[8,128,256]{2,1,0:T(8,128)(2,1)S(1)}, u32[]{:S(2)}, u32[]{:S(2)}) collective-permute-start(bf16[8,128,256]{2,1,0:T(8,128)(2,1)S(1)} %bitcast.35), channel_id=1, source_target_pairs={{0,32},{32,0},{1,33},{33,1},{2,34},{34,2},{3,35},{35,3},{4,36},{36... | collective-permute-start | bytes 1572872 | tf_op jit(solution)/shard_map/ppermute | solution.py:183
  46.1 0.0 copy-start
  46.1 1.5 %collective-permute-done = bf16[8,128,256]{2,1,0:T(8,128)(2,1)S(1)} collective-permute-done((bf16[8,128,256]{2,1,0:T(8,128)(2,1)S(1)}, bf16[8,128,256]{2,1,0:T(8,128)(2,1)S(1)}, u32[]{:S(2)}, u32[]{:S(2)}) %collective-permute-start) | collective-permute-done | bytes 524320 | tf_op jit(solution)/shard_map/ppermute | solution.py:183
  47.6 0.1 select_bitcast_fusion.1
  47.7 0.1 pad_maximum_fusion
  47.8 0.0 copy-start.2
  47.8 0.0 copy-start.3
  47.8 0.4 copy-done
  48.3 1.8 %shard_map.68 = bf16[1024,256]{1,0:T(8,128)(2,1)S(1)} custom-call(bf16[1024,2048]{1,0:T(8,128)(2,1)S(1)} %copy-done, bf16[2048,256]{1,0:T(8,128)(2,1)S(1)} %bitcast.31), custom_call_target="tpu_custom_call" | custom-call | flops 1073741824 | bytes 4194304 | tf_op jit(solution)/shard_map/pallas_call | solution.py:54
  50.0 24.6 %all_to_all.37 = bf16[8,128,256]{2,1,0:T(8,128)(2,1)S(1)} all-to-all(bf16[8,128,256]{2,1,0:T(8,128)(2,1)S(1)} %bitcast.32), channel_id=1, replica_groups=mesh['x'=4,'zh'=2,'core'=2,'primal'=8,'seq'=4] {'primal'}, dimensions={0} | all-to-all | bytes 1048576 | tf_op jit(solution)/shard_map/all_to_all | solution.py:22
  74.6 0.1 reduce_sum.46
  74.7 9.6 %all_to_all.38.gradient_ref = bf16[4,128,256]{2,1,0:T(8,128)(2,1)S(1)} all-to-all(bf16[4,128,256]{2,1,0:T(8,128)(2,1)S(1)} %broadcast_in_dim.34), channel_id=1, replica_groups=mesh['x'=4,'zh'=2,'core'=2,'primal'=8,'seq'=4] {'seq'}, dimensions={0} | all-to-all | bytes 524288 | tf_op jit(solution)/shard_map/all_to_all | solution.py:22
  84.3 0.0 copy-done.2
  84.3 0.0 copy-done.3
  84.3 0.0 copy-start.1
  84.3 1.5 %shard_map.69 = (bf16[8,256,128]{2,1,0:T(8,128)(2,1)S(1)}, f32[128,256]{1,0:T(8,128)}) custom-call(s32[1]{0:T(128)} %bitcast.10.seq_ref, bf16[4,128,256]{2,1,0:T(8,128)(2,1)S(1)} %all_to_all.38.gradient_ref, bf16[1024,256]{1,0:T(8,128)(2,1)S(1)} %copy-done.2, s32[1,1024]{1,0:T(1,128)S(1)} %bitcast.34), custom_call_target="tpu_custom_call" | custom-call | flops 2147483648 | bytes 524288 | tf_op jit(solution)/shard_map/pallas_call | solution.py:146
  85.8 16.8 %all_to_all.39.block_ref = bf16[8,256,128]{2,1,0:T(8,128)(2,1)S(1)} all-to-all(bf16[8,256,128]{2,1,0:T(8,128)(2,1)S(1)} %get-tuple-element.17), channel_id=1, replica_groups=mesh['x'=4,'zh'=2,'core'=2,'primal'=8,'seq'=4] {'primal'}, dimensions={0} | all-to-all | bytes 1048576 | tf_op jit(solution)/shard_map/all_to_all | solution.py:22
  102.6 0.0 copy-done.1
  102.7 1.7 %shard_map.71 = bf16[2,4,256,128]{3,2,1,0:T(8,128)(2,1)S(1)} custom-call(s32[1]{0:T(128)} %bitcast.14.core_ref, bf16[1024,2048]{1,0:T(8,128)(2,1)S(1)} %copy-done.1, bf16[8,256,128]{2,1,0:T(8,128)(2,1)S(1)} %all_to_all.39.block_ref), custom_call_target="tpu_custom_call" | custom-call | flops 536870912 | bytes 2097152 | tf_op jit(solution)/shard_map/pallas_call | solution.py:93
  104.3 5.9 %collective-permute-start.1 = (bf16[2,4,256,128]{3,2,1,0:T(8,128)(2,1)S(1)}, bf16[2,4,256,128]{3,2,1,0:T(8,128)(2,1)S(1)}, u32[]{:S(2)}, u32[]{:S(2)}) collective-permute-start(bf16[2,4,256,128]{3,2,1,0:T(8,128)(2,1)S(1)} %shard_map.71), channel_id=1, source_target_pairs={{0,32},{32,0},{1,33},{33,1},{2,34},{34,2},{3,35},{35,3},{4,36},{36... | collective-permute-start | bytes 1572872 | tf_op jit(solution)/shard_map/ppermute | solution.py:200
  110.3 1.7 %shard_map.70 = bf16[2,4,256,128]{3,2,1,0:T(8,128)(2,1)S(1)} custom-call(s32[1]{0:T(128)} %bitcast.13.core_ref, bf16[1024,2048]{1,0:T(8,128)(2,1)S(1)} %copy-done.1, bf16[8,256,128]{2,1,0:T(8,128)(2,1)S(1)} %all_to_all.39.block_ref), custom_call_target="tpu_custom_call" | custom-call | flops 536870912 | bytes 2097152 | tf_op jit(solution)/shard_map/pallas_call | solution.py:93
  112.0 0.0 collective-permute-done.1
  112.0 0.1 add_convert_fusion
  112.1 0.7 select_bitcast_fusion.2
  112.9 8.8 %all_to_all.40 = bf16[4,256,128]{2,1,0:T(8,128)(2,1)S(1)} all-to-all(bf16[4,256,128]{2,1,0:T(8,128)(2,1)S(1)} %get-tuple-element.29), channel_id=1, replica_groups=mesh['x'=4,'zh'=2,'core'=2,'primal'=8,'seq'=4] {'x'}, dimensions={0} | all-to-all | bytes 524288 | tf_op jit(solution)/shard_map/all_to_all | solution.py:22
  121.7 3.4 %all-to-all-start.6 = ((bf16[4,256,128]{2,1,0:T(8,128)(2,1)}), bf16[4,256,128]{2,1,0:T(8,128)(2,1)S(1)}, u32[]{:S(2)}, u32[]{:S(2)}) async-start(bf16[4,256,128]{2,1,0:T(8,128)(2,1)} %get-tuple-element.20), calls=%async_computation.6 | async-start | bytes 524288 | tf_op jit(solution)/shard_map/all_to_all | solution.py:22
  125.1 3.5 %collective-permute-start.2 = (bf16[256,128]{1,0:T(8,128)(2,1)S(1)}, bf16[256,128]{1,0:T(8,128)(2,1)S(1)}, u32[]{:S(2)}, u32[]{:S(2)}) collective-permute-start(bf16[256,128]{1,0:T(8,128)(2,1)S(1)} %reduce_sum.48), channel_id=1, source_target_pairs={{0,64},{64,0},{1,65},{65,1},{2,66},{66,2},{3,67},{67,3},{4,68},{68... | collective-permute-start | bytes 196616 | tf_op jit(solution)/shard_map/ppermute | solution.py:205
  128.6 2.0 %all-to-all-done.6 = bf16[4,256,128]{2,1,0:T(8,128)(2,1)S(1)} async-done(((bf16[4,256,128]{2,1,0:T(8,128)(2,1)}), bf16[4,256,128]{2,1,0:T(8,128)(2,1)S(1)}, u32[]{:S(2)}, u32[]{:S(2)}) %all-to-all-start.6) | async-done | bytes 262176 | tf_op jit(solution)/shard_map/all_to_all | solution.py:22
  130.6 4.2 %collective-permute-done.2 = bf16[256,128]{1,0:T(8,128)(2,1)S(1)} collective-permute-done((bf16[256,128]{1,0:T(8,128)(2,1)S(1)}, bf16[256,128]{1,0:T(8,128)(2,1)S(1)}, u32[]{:S(2)}, u32[]{:S(2)}) %collective-permute-start.2) | collective-permute-done | bytes 65568 | tf_op jit(solution)/shard_map/ppermute | solution.py:205
  134.9 0.8 copy.11
  (6 shorter events, 0.2 us)
Async XLA Ops:
  40.3 7.3 %collective-permute-start = (bf16[8,128,256]{2,1,0:T(8,128)(2,1)S(1)}, bf16[8,128,256]{2,1,0:T(8,128)(2,1)S(1)}, u32[]{:S(2)}, u32[]{:S(2)}) collective-permute-start(bf16[8,128,256]{2,1,0:T(8,128)(2,1)S(1)} %bitcast.35), channel_id=1, source_target_pairs={{0,32},{32,0},{1,33},{33,1},{2,34},{34,2},{3,35},{35,3},{4,36},{36... | collective-permute-start | bytes 1572872 | tf_op jit(solution)/shard_map/ppermute | solution.py:183
  46.1 2.2 %copy-start = (bf16[1024,2048]{1,0:T(8,128)(2,1)S(1)}, bf16[1024,2048]{1,0:T(8,128)(2,1)}, u32[]{:S(2)}) copy-start(bf16[1024,2048]{1,0:T(8,128)(2,1)} %payoff_ref.5) | copy-start | bytes 12582916
  47.8 36.5 %copy-start.2 = (bf16[1024,256]{1,0:T(8,128)(2,1)S(1)}, bf16[1024,256]{1,0:T(8,128)(2,1)}, u32[]{:S(2)}) copy-start(bf16[1024,256]{1,0:T(8,128)(2,1)} %seq_payoff_ref.1) | copy-start | bytes 1572868
  47.8 36.5 %copy-start.3 = (s32[1024]{0:T(1024)S(1)}, s32[1024]{0:T(1024)}, u32[]{:S(2)}) copy-start(s32[1024]{0:T(1024)} %param.9) | copy-start | bytes 12292
  84.3 18.3 %copy-start.1 = (bf16[1024,2048]{1,0:T(8,128)(2,1)S(1)}, bf16[1024,2048]{1,0:T(8,128)(2,1)}, u32[]{:S(2)}) copy-start(bf16[1024,2048]{1,0:T(8,128)(2,1)} %payoff_ref.5) | copy-start | bytes 12582916
  104.3 7.6 %collective-permute-start.1 = (bf16[2,4,256,128]{3,2,1,0:T(8,128)(2,1)S(1)}, bf16[2,4,256,128]{3,2,1,0:T(8,128)(2,1)S(1)}, u32[]{:S(2)}, u32[]{:S(2)}) collective-permute-start(bf16[2,4,256,128]{3,2,1,0:T(8,128)(2,1)S(1)} %shard_map.71), channel_id=1, source_target_pairs={{0,32},{32,0},{1,33},{33,1},{2,34},{34,2},{3,35},{35,3},{4,36},{36... | collective-permute-start | bytes 1572872 | tf_op jit(solution)/shard_map/ppermute | solution.py:200
  121.7 8.9 %all-to-all-start.6 = ((bf16[4,256,128]{2,1,0:T(8,128)(2,1)}), bf16[4,256,128]{2,1,0:T(8,128)(2,1)S(1)}, u32[]{:S(2)}, u32[]{:S(2)}) async-start(bf16[4,256,128]{2,1,0:T(8,128)(2,1)} %get-tuple-element.20), calls=%async_computation.6 | async-start | bytes 524288 | tf_op jit(solution)/shard_map/all_to_all | solution.py:22
  125.1 9.7 %collective-permute-start.2 = (bf16[256,128]{1,0:T(8,128)(2,1)S(1)}, bf16[256,128]{1,0:T(8,128)(2,1)S(1)}, u32[]{:S(2)}, u32[]{:S(2)}) collective-permute-start(bf16[256,128]{1,0:T(8,128)(2,1)S(1)} %reduce_sum.48), channel_id=1, source_target_pairs={{0,64},{64,0},{1,65},{65,1},{2,66},{66,2},{3,67},{67,3},{4,68},{68... | collective-permute-start | bytes 196616 | tf_op jit(solution)/shard_map/ppermute | solution.py:205
